TPU v7x, 512 devices: a whole 4x8x8 slice. The times are simulated.
512 devices in a mesh: section: 16 (over y, z_hi), replica: 4 (over x), tensor: 8 (over z_lo, core).
Axes of the slice: x: 4, y: 8, z: 8 (z_hi: 2, z_lo: 4; z = z_hi * 4 + z_lo), core: 2. Of those that a mesh axis runs over, the one named last changes fastest.
Arguments:
- act_log: bfloat16 [16, 1024, 5120], P('section', 'replica', 'tensor'), may hold values from -16 to 16
- grad_log: bfloat16 [16, 1024, 5120], P('section', 'replica', 'tensor'), may hold values from -16 to 16
- failed_section: int32 [16], replicated, may hold values from 0 to 15, each once
- live_tokens: int32 [4], replicated, may hold values from 1 to 256, 768 in all
- gate_weight: bfloat16 [5120, 13824], P('tensor', ('section', 'replica')), may hold values from -0.078125 to 0.078125
- up_weight: bfloat16 [5120, 13824], P('tensor', ('section', 'replica')), may hold values from -0.078125 to 0.078125
- down_weight: bfloat16 [13824, 5120], P(('section', 'replica'), 'tensor'), may hold values from -0.0546875 to 0.0546875
- norm_gain: bfloat16 [5120], P('tensor'), may hold values from 0.099609375 to 1.8984375
Outputs:
- d_input: bfloat16 [1024, 5120], P(('section', 'replica'), 'tensor')
- grad_gate: bfloat16 [5120, 13824], P('tensor', ('section', 'replica'))
- grad_up: bfloat16 [5120, 13824], P('tensor', ('section', 'replica'))
- grad_down: bfloat16 [13824, 5120], P(('section', 'replica'), 'tensor')
- grad_gain: float32 [5120], P('tensor')
Inputs may be any that keep to these rules, and one draw needn't show every extreme that they name: `failed_section`: each section index appears exactly once. `live_tokens`: the entries sum to 768 and some micro-batch is full.
All inputs are finite; a program needn't handle non-finite values.
Results may differ from a plain program's by a relative error of at most 0.027.
Values may be sent and summed in bfloat16 or wider, within the bound.
No kernel may reach another device: no remote copies, remote signals or barrier semaphores. Data moves between devices by JAX's collectives and lax.ppermute only.
A program may use at most 64 MiB of HBM per device.

v0:
```python
import functools

import jax
import jax.numpy as jnp
from jax import lax
from jax.experimental import pallas as pl
from jax.experimental.pallas import tpu as pltpu
from jax.sharding import Mesh, PartitionSpec as P

AXES = ("y", "zh", "x", "zl", "c")
ROWS_AXES = ("y", "zh", "x")
F32 = jnp.float32
BF16 = jnp.bfloat16
WIDE = 256
VMEM = pl.BlockSpec(memory_space=pltpu.VMEM)
SMEM = pl.BlockSpec(memory_space=pltpu.SMEM)


def contract(left, right, l, r):
    return lax.dot_general(left, right, (((l,), (r,)), ((), ())), preferred_element_type=F32)


def call(body, outs, scratch, flops, *args):
    moved = sum(a.size * a.dtype.itemsize for a in args) + sum(
        o.size * o.dtype.itemsize for o in jax.tree.leaves(outs)
    )
    return pl.pallas_call(
        body,
        out_shape=outs,
        in_specs=[SMEM if a.ndim == 1 else VMEM for a in args],
        out_specs=jax.tree.map(lambda _: VMEM, outs),
        scratch_shapes=scratch,
        compiler_params=pltpu.CompilerParams(vmem_limit_bytes=48 * 1024 * 1024),
        cost_estimate=pl.CostEstimate(flops=flops, bytes_accessed=moved, transcendentals=0),
    )(*args)


def pick(refs, k):
    own, right, left, over_in, over_up = refs
    if k < 3:
        ref = (own, right, left)[k]
        return ref[0], ref[1]
    return over_in[...], over_up[...]


def log2(n):
    assert n & (n - 1) == 0
    return n.bit_length() - 1


CORE, REPLICA, ME, LINE, LIVE = 0, 1, 2, 3, 4


def scatter_kernel(per, live, act, grad, send):
    tokens = act.shape[1]
    x = lax.axis_index("x")
    off = jnp.int32(0)
    for b in range(live.shape[0] - 1):
        off = off + jnp.where(x > b, live[b], 0)
    shape = (2 * tokens, tokens)
    row = lax.broadcasted_iota(jnp.int32, shape, 0)
    column = lax.broadcasted_iota(jnp.int32, shape, 1)
    place = (row >> log2(2 * per) << log2(per)) + (row & (per - 1))
    hot = ((place - (off & (tokens - 1)) + tokens) & (tokens - 1)) == column
    is_up = (row & per) != 0
    first = jnp.where(hot & ~is_up, 1.0, 0.0).astype(BF16)
    second = jnp.where(hot & is_up, 1.0, 0.0).astype(BF16)
    send[...] = (contract(first, act[0], 1, 0) + contract(second, grad[0], 1, 0)).astype(BF16)


def terms_kernel(hid, nums, own, right, left, over_in, over_up, gain, gate, up, down, keep, send):
    core = nums[CORE]
    gain_wide = gain[...].astype(F32)
    for k in range(4):
        inputs, upstream = pick((own, right, left, over_in, over_up), k)
        n = inputs.shape[0]
        wide = inputs.astype(F32)
        squares = jnp.sum(wide * wide, axis=1, keepdims=True)
        sq_hi = squares.astype(BF16).astype(F32)
        scaled = (wide * gain_wide).astype(BF16)
        lane = lax.broadcasted_iota(jnp.int32, (n, WIDE), 1)
        first = contract(scaled, gate[...], 1, 1)
        first = jnp.where(lane == hid, sq_hi, jnp.where(lane == hid + 1, squares - sq_hi, first))
        parts = (
            first.astype(BF16),
            contract(scaled, up[...], 1, 1).astype(BF16),
            contract(upstream, down[...], 1, 1).astype(BF16),
        )
        at = (k % 2) * n

        def store(out):
            for i, part in enumerate(parts):
                out[at : at + n, i * WIDE : (i + 1) * WIDE] = part

        pl.when(core == k // 2)(functools.partial(store, keep))
        pl.when(core != k // 2)(functools.partial(store, send))


def pair_kernel(nums, keep, recv, *outs):
    own = outs[0].shape[0]
    for i, out in enumerate(outs):
        chunk = (nums[LINE] + i) & (len(outs) - 1)
        rows = pl.ds(pl.multiple_of(chunk * own, own), own)
        out[...] = (keep[rows, :].astype(F32) + recv[rows, :].astype(F32)).astype(BF16)


def point_kernel(hid, features, *refs):
    terms, out = refs[:-1], refs[-1]

    def total(i):
        s = slice(i * WIDE, (i + 1) * WIDE)
        return sum((t[:, s].astype(F32) for t in terms[1:]), terms[0][:, s].astype(F32))

    gate, up, hidden_grad = total(0), total(1), total(2)
    lane = lax.broadcasted_iota(jnp.int32, gate.shape, 1)
    squares = jnp.sum(jnp.where((lane == hid) | (lane == hid + 1), gate, 0.0), axis=1, keepdims=True)
    inv_rms = lax.rsqrt(squares / features + 1e-05)
    gate = jnp.where(lane < hid, gate, 0.0) * inv_rms
    up = up * inv_rms
    logistic = jax.nn.sigmoid(gate)
    swished = gate * logistic
    slopes = logistic * (1.0 + gate * (1.0 - logistic))
    hidden = swished * up
    d_gate = (hidden_grad * up * slopes).astype(BF16)
    d_up = (hidden_grad * swished).astype(BF16)
    inner = jnp.sum(d_gate.astype(F32) * gate + d_up.astype(F32) * up, axis=1, keepdims=True)
    lane = lax.broadcasted_iota(jnp.int32, (gate.shape[0], 4), 1)
    inv_hi = inv_rms.astype(BF16).astype(F32)
    in_hi = inner.astype(BF16).astype(F32)
    tail = jnp.where(
        lane == 0, inv_hi, jnp.where(lane == 1, inv_rms - inv_hi, jnp.where(lane == 2, in_hi, inner - in_hi))
    )
    out[:, :hid] = hidden[:, :hid].astype(BF16)
    out[:, hid : 2 * hid] = d_gate[:, :hid]
    out[:, 2 * hid : 3 * hid] = d_up[:, :hid]
    out[:, 3 * hid :] = tail.astype(BF16)


def rows_of(every, k, n):
    cores, own = 2, n // 2
    at = [(((k % 2) * 2 + j) * cores + k // 2) * own for j in range(2)]
    return jnp.concatenate([every[a : a + own, :] for a in at], axis=0)


def where_packed(nums, row, batches, tokens, per, nx, block, part):
    batch = row >> log2(tokens)
    slot = row & (tokens - 1)
    limit, off = jnp.zeros_like(row), jnp.zeros_like(row)
    for b in range(batches):
        limit = jnp.where(batch == b, nums[LIVE + b], limit)
        off = jnp.where(batch == b, nums[LIVE + batches + b], off)
    at = off + slot
    device = (at & (tokens - 1)) >> log2(per)
    turn = (device - nums[REPLICA] + nx) & (nx - 1)
    held = jnp.where(turn == nx - 1, 1, jnp.where(turn == 1, 2, jnp.where(turn == 2, 3, 0)))
    index = held * part + (device >> log2(nx)) * block + (at >> log2(tokens)) * per + (at & (per - 1))
    return jnp.where(slot < limit, index, -1)


def term_kernel(
    hid, features, plan, nums, own, right, left, over_in, over_up, every, gain, gate, up,
    out, up_own, term_ref,
):
    nx = out.shape[0]
    gain_wide = gain[...].astype(F32)
    gain_term = jnp.zeros(gain_wide.shape, F32)
    own_rows = up_own.shape[0]
    own_total = jnp.zeros(up_own.shape, F32)
    row = nums[ME] * own_rows + lax.broadcasted_iota(jnp.int32, (own_rows, 1), 0)
    index = where_packed(nums, row, *plan)
    for k in range(4):
        inputs, upstream = pick((own, right, left, over_in, over_up), k)
        n = inputs.shape[0]
        pay = rows_of(every, k, n)
        tail = pay[:, 3 * hid :].astype(F32)
        inv_rms = tail[:, 0:1] + tail[:, 1:2]
        inner = tail[:, 2:3] + tail[:, 3:4]
        d_normed = contract(pay[:, hid : 2 * hid], gate[...], 1, 0) + contract(
            pay[:, 2 * hid : 3 * hid], up[...], 1, 0
        )
        unit = inputs.astype(F32) * inv_rms
        gain_term = gain_term + jnp.sum(d_normed * unit, axis=0, keepdims=True)
        term = inv_rms * (gain_wide * d_normed - unit * (inner / features))
        term_ref[k * n : (k + 1) * n, :] = term.astype(BF16)
        column = lax.broadcasted_iota(jnp.int32, (own_rows, n), 1) + k * n
        hot = jnp.where(index == column, 1.0, 0.0).astype(BF16)
        own_total = own_total + contract(hot, upstream, 1, 0)
    up_own[...] = own_total.astype(BF16)
    gain_hi = gain_term.astype(BF16).astype(F32)
    rows = plan[0] * plan[1] // nx
    extra = out.shape[1] - rows
    row = lax.broadcasted_iota(jnp.int32, (extra, gain_term.shape[1]), 0)
    extras = jnp.where(row == 0, gain_hi, jnp.where(row == 1, gain_term - gain_hi, 0.0)).astype(BF16)
    live = term_ref.shape[0]
    column = lax.broadcasted_iota(jnp.int32, (rows, live), 1)
    i = lax.broadcasted_iota(jnp.int32, (rows, 1), 0)
    for q in range(nx):
        row = (((i >> log2(own_rows)) * nx + q) << log2(own_rows)) + (i & (own_rows - 1))
        hot = jnp.where(where_packed(nums, row, *plan) == column, 1.0, 0.0).astype(BF16)
        out[q, :rows, :] = contract(hot, term_ref[...], 1, 0).astype(BF16)
        out[q, rows:, :] = extras


def grads_kernel(
    hid, own, right, left, over_in, over_up, every, gain,
    grad_gate, grad_up, grad_down, pay_ref, normed_ref, up_ref,
):
    gain_wide = gain[...].astype(F32)
    for k in range(4):
        inputs, upstream = pick((own, right, left, over_in, over_up), k)
        n = inputs.shape[0]
        s = slice(k * n, (k + 1) * n)
        pay = rows_of(every, k, n)
        tail = pay[:, 3 * hid :].astype(F32)
        inv_rms = tail[:, 0:1] + tail[:, 1:2]
        for i in range(3):
            pay_ref[i, s, :hid] = pay[:, i * hid : (i + 1) * hid]
        normed_ref[s, :] = (inputs.astype(F32) * inv_rms * gain_wide).astype(BF16)
        up_ref[s, :] = upstream
    grad_down[...] = contract(pay_ref[0, :, :hid], up_ref[...], 0, 0).astype(BF16)
    normed = normed_ref[...]
    grad_gate[...] = contract(pay_ref[1, :, :hid], normed, 0, 0).astype(BF16)
    grad_up[...] = contract(pay_ref[2, :, :hid], normed, 0, 0).astype(BF16)


def middle_kernel(parts, out):
    sections, own_rows, lanes = out.shape
    width = parts.shape[2]
    rows = sections * own_rows
    total = parts[0].astype(F32)
    for r in range(1, parts.shape[0]):
        total = total + parts[r].astype(F32)
    out[:, :, :width] = total[:rows].astype(BF16).reshape(sections, own_rows, width)
    gain = total[rows : rows + 1] + total[rows + 1 : rows + 2]
    row = lax.broadcasted_iota(jnp.int32, (own_rows, 128), 0)
    tile = jnp.zeros((own_rows, 128), F32)
    for i in range(width // 128):
        tile = jnp.where(row == i, gain[:, i * 128 : (i + 1) * 128], tile)
    tile = tile.astype(BF16)
    for s in range(sections):
        out[s, :, width:] = tile


def final_kernel(parts, up_own, d_input, grad_gain):
    width = up_own.shape[1]
    total = parts[0].astype(F32)
    for r in range(1, parts.shape[0]):
        total = total + parts[r].astype(F32)
    d_input[...] = (up_own[...].astype(F32) + total[:, :width]).astype(BF16)
    for i in range(width // 128):
        grad_gain[:, i * 128 : (i + 1) * 128] = total[i : i + 1, width:]


def per_device(
    act_log, grad_log, failed_section, live_tokens, gate_weight, up_weight, down_weight, norm_gain
):
    ny, nzh, nx = (lax.axis_size(a) for a in ROWS_AXES)
    nzl, nc = lax.axis_size("zl"), lax.axis_size("c")
    sections = ny * nzh
    shards = sections * nx
    tokens, width = act_log.shape[1:]
    batches = live_tokens.shape[0]
    rows = batches * tokens
    live = 3 * rows // 4
    per = tokens // (ny * nx)
    cycles = live // tokens
    features = float(width * nzl * nc)
    hid = gate_weight.shape[1]
    failed = failed_section[0]
    source = (failed + sections - 1) % sections
    target = (failed + 1) % sections
    batch = jnp.arange(batches, dtype=jnp.int32)
    offs = jnp.sum(jnp.where(batch[None, :] < batch[:, None], live_tokens[None, :], 0), axis=1)
    x = lax.axis_index("x")
    me = lax.axis_index(ROWS_AXES)
    plan = (batches, tokens, per, nx, cycles * per, ny * cycles * per)

    def shape(*dims, dtype=BF16):
        return jax.ShapeDtypeStruct(dims, dtype)

    nums = jnp.stack([lax.axis_index("c"), x, me, lax.axis_index("zl")]).astype(jnp.int32)
    nums = jnp.concatenate([nums, live_tokens, offs.astype(jnp.int32)])
    send = call(
        functools.partial(scatter_kernel, per), shape(2 * tokens, width), [],
        4 * tokens * tokens * width, live_tokens, act_log, grad_log,
    )
    recv = lax.all_to_all(send, ("y", "x"), 0, 0, tiled=True).reshape(ny * nx, 2 * per, width)
    got = jnp.stack(
        [
            lax.dynamic_slice_in_dim(recv, source // nzh * nx, nx, 0)[:, :per],
            lax.dynamic_slice_in_dim(recv, target // nzh * nx, nx, 0)[:, per:],
        ]
    )
    place = lax.axis_index(("y", "x")) * per + jnp.arange(per, dtype=jnp.int32)
    slot = (place[None, :] - offs[:, None]) % tokens
    cycle = (offs[:, None] + slot) // tokens
    hit = (slot < live_tokens[:, None])[:, None, :] & (
        cycle[:, None, :] == jnp.arange(cycles, dtype=jnp.int32)[None, :, None]
    )
    packed = jnp.sum(
        jnp.where(hit[None, :, :, :, None], got[:, :, None].astype(F32), 0.0), axis=1
    ).astype(BF16)
    block = cycles * per
    packed = packed.reshape(2 * block, width)

    other = lax.ppermute(packed, "zh", [(0, 1), (1, 0)])
    packed = jnp.where(lax.axis_index("zh") == source % nzh, packed, other)

    copies = jnp.broadcast_to(packed[None], (ny,) + packed.shape).reshape(-1, width)
    column = lax.all_to_all(copies, "y", 0, 0, tiled=True)
    part = ny * block
    out_row = lax.broadcasted_iota(jnp.int32, (2 * part, 2 * part), 0)
    from_row = lax.broadcasted_iota(jnp.int32, (2 * part, 2 * part), 1)
    at = out_row % part
    hot = (at // block * 2 + out_row // part) * block + at % block == from_row
    own = contract(hot.astype(BF16), column, 1, 0).astype(BF16).reshape(2, part, width)
    ahead = [(i, (i + 1) % nx) for i in range(nx)]
    back = [(i, (i - 1) % nx) for i in range(nx)]
    right = lax.ppermute(own, "x", ahead)
    left = lax.ppermute(own, "x", back)
    over_in = lax.ppermute(right[0], "x", ahead)
    over_up = lax.ppermute(left[1], "x", back)
    blocks = (own, right, left, over_in, over_up)

    pad = ((0, WIDE - hid), (0, 0))
    gate_rows, up_rows = gate_weight.T, up_weight.T
    gate_pad, up_pad, down_pad = (jnp.pad(w, pad) for w in (gate_rows, up_rows, down_weight))
    gain = norm_gain.reshape(1, width)
    lanes = 3 * WIDE
    half = live // nc
    own_count = half // nzl

    product = 2 * live * width * WIDE
    keep, give = call(
        functools.partial(terms_kernel, hid), (shape(half, lanes), shape(half, lanes)), [], 3 * product,
        nums, *blocks, gain, gate_pad, up_pad, down_pad,
    )
    taken = lax.ppermute(give, "c", [(0, 1), (1, 0)])
    chunk = shape(own_count, lanes)
    pairs = call(pair_kernel, (chunk,) * nzl, [], half * lanes, nums, keep, taken)
    others = [
        lax.ppermute(pairs[i], "zl", [(a, (a + i) % nzl) for a in range(nzl)]) for i in range(1, nzl)
    ]
    point = call(
        functools.partial(point_kernel, hid, features), shape(own_count, 3 * hid + 4), [],
        20 * own_count * lanes, pairs[0], *others,
    )
    every = lax.all_gather(point, ("zl", "c"), axis=0, tiled=True)

    own_rows = rows // shards
    count = rows // nx
    out, up_own = call(
        functools.partial(term_kernel, hid, features, plan),
        (shape(nx, count + 16, width), shape(own_rows, width)),
        [pltpu.VMEM((live, width), BF16)],
        5 * product,
        nums, *blocks, every, gain, gate_rows, up_rows,
    )
    out = lax.all_to_all(out, "x", 0, 0, tiled=True)
    out = call(
        middle_kernel, shape(sections, own_rows, width + 128), [], nx * count * width, out
    )
    out = lax.all_to_all(out, ("y", "zh"), 0, 0, tiled=True)
    d_input, grad_gain = call(
        final_kernel, (shape(own_rows, width), shape(1, width, dtype=F32)), [],
        sections * own_rows * width, out, up_own,
    )

    grad_gate, grad_up, grad_down = call(
        functools.partial(grads_kernel, hid),
        (shape(hid, width),) * 3,
        [
            pltpu.VMEM((3, live, WIDE), BF16),
            pltpu.VMEM((live, width), BF16),
            pltpu.VMEM((live, width), BF16),
        ],
        3 * product,
        *blocks, every, gain,
    )
    return (d_input, grad_gate.T, grad_up.T, grad_down, grad_gain.reshape(width))


def solution(mesh):
    fine = Mesh(mesh.devices.reshape(8, 2, 4, 4, 2), AXES)
    section, replica, tensor = ("y", "zh"), "x", ("zl", "c")
    split = ("y", "zh", "x")
    in_specs = (
        P(section, replica, tensor),
        P(section, replica, tensor),
        P(),
        P(),
        P(tensor, split),
        P(tensor, split),
        P(split, tensor),
        P(tensor),
    )
    out_specs = (
        P(split, tensor),
        P(tensor, split),
        P(tensor, split),
        P(split, tensor),
        P(tensor),
    )
    return jax.shard_map(
        per_device, mesh=fine, in_specs=in_specs, out_specs=out_specs, check_vma=False
    )
```

profile of v0, /device:TPU:1, one launch (start us, length us, event | category | flops | bytes accessed | tf_op | source)
XLA Modules:
  0.0 192.0 jit_solution(7608018212516146981)
XLA Ops:
  3.2 2.0 %shard_map.119 = bf16[512,640]{1,0:T(8,128)(2,1)} custom-call(s32[4]{0:T(128)S(1)} %copy-done.8, bf16[1,256,640]{2,1,0:T(8,128)(2,1)S(1)} %copy-done, bf16[1,256,640]{2,1,0:T(8,128)(2,1)S(1)} %copy-done.1), custom_call_target="tpu_custom_call" | custom-call | flops 167772160 | bytes 1310736 | tf_op jit(solution)/shard_map/pallas_call | solution.py:27
  5.2 10.5 %all-to-all-start = ((bf16[32,16,640]{2,1,0:T(8,128)(2,1)}), bf16[32,16,640]{2,1,0:T(8,128)(2,1)S(1)}, u32[]{:S(2)}, u32[]{:S(2)}) async-start(bf16[32,16,640]{2,1,0:T(8,128)(2,1)} %bitcast.5), calls=%async_computation | async-start | bytes 1310720 | tf_op jit(solution)/shard_map/all_to_all | solution.py:287
  16.2 18.2 %all-to-all-done = bf16[32,16,640]{2,1,0:T(8,128)(2,1)S(1)} async-done(((bf16[32,16,640]{2,1,0:T(8,128)(2,1)}), bf16[32,16,640]{2,1,0:T(8,128)(2,1)S(1)}, u32[]{:S(2)}, u32[]{:S(2)}) %all-to-all-start) | async-done | bytes 655392 | tf_op jit(solution)/shard_map/all_to_all | solution.py:287
  34.5 10.7 %collective-permute-start = (bf16[48,640]{1,0:T(8,128)(2,1)S(1)}, bf16[48,640]{1,0:T(8,128)(2,1)S(1)}, u32[]{:S(2)}, u32[]{:S(2)}) collective-permute-start(bf16[48,640]{1,0:T(8,128)(2,1)S(1)} %bitcast.35), channel_id=1, source_target_pairs={{0,32},{32,0},{1,33},{33,1},{2,34},{34,2},{3,35},{35,3},{4,36},{36... | collective-permute-start | bytes 184328 | tf_op jit(solution)/shard_map/ppermute | solution.py:306
  47.7 3.5 %all-to-all-start.1 = ((bf16[8,48,640]{2,1,0:T(8,128)(2,1)}), bf16[8,48,640]{2,1,0:T(8,128)(2,1)S(1)}, u32[]{:S(2)}, u32[]{:S(2)}) async-start(bf16[8,48,640]{2,1,0:T(8,128)(2,1)} %broadcast_in_dim.55), calls=%async_computation.1 | async-start | bytes 983040 | tf_op jit(solution)/shard_map/all_to_all | solution.py:310
  51.2 12.6 %all-to-all-done.1 = bf16[8,48,640]{2,1,0:T(8,128)(2,1)S(1)} async-done(((bf16[8,48,640]{2,1,0:T(8,128)(2,1)}), bf16[8,48,640]{2,1,0:T(8,128)(2,1)S(1)}, u32[]{:S(2)}, u32[]{:S(2)}) %all-to-all-start.1) | async-done | bytes 491552 | tf_op jit(solution)/shard_map/all_to_all | solution.py:310
  64.9 3.5 %collective-permute-start.1 = (bf16[2,192,640]{2,1,0:T(8,128)(2,1)S(1)}, bf16[2,192,640]{2,1,0:T(8,128)(2,1)S(1)}, u32[]{:S(2)}, u32[]{:S(2)}) collective-permute-start(bf16[2,192,640]{2,1,0:T(8,128)(2,1)S(1)} %bitcast.25), channel_id=1, source_target_pairs={{0,8},{8,16},{16,24},{24,0},{1,9},{9,17},{17,25},{25,1},{2,10},{10... | collective-permute-start | bytes 1474568 | tf_op jit(solution)/shard_map/ppermute | solution.py:319
  68.5 3.5 %collective-permute-start.2 = (bf16[2,192,640]{2,1,0:T(8,128)(2,1)S(1)}, bf16[2,192,640]{2,1,0:T(8,128)(2,1)S(1)}, u32[]{:S(2)}, u32[]{:S(2)}) collective-permute-start(bf16[2,192,640]{2,1,0:T(8,128)(2,1)S(1)} %bitcast.26), channel_id=1, source_target_pairs={{0,24},{8,0},{16,8},{24,16},{1,25},{9,1},{17,9},{25,17},{2,26},{10... | collective-permute-start | bytes 1474568 | tf_op jit(solution)/shard_map/ppermute | solution.py:320
  72.0 4.7 %collective-permute-done.1.right = bf16[2,192,640]{2,1,0:T(8,128)(2,1)S(1)} collective-permute-done((bf16[2,192,640]{2,1,0:T(8,128)(2,1)S(1)}, bf16[2,192,640]{2,1,0:T(8,128)(2,1)S(1)}, u32[]{:S(2)}, u32[]{:S(2)}) %collective-permute-start.1) | collective-permute-done | bytes 491552 | tf_op jit(solution)/shard_map/ppermute | solution.py:319
  77.4 2.0 %collective-permute-start.3 = (bf16[192,640]{1,0:T(8,128)(2,1)}, bf16[192,640]{1,0:T(8,128)(2,1)S(1)}, u32[]{:S(2)}, u32[]{:S(2)}) collective-permute-start(bf16[192,640]{1,0:T(8,128)(2,1)} %slice_bitcast_fusion.1), channel_id=1, source_target_pairs={{0,8},{8,16},{16,24},{24,0},{1,9},{9,17},{17,25},{25,1},{2,10},{10... | collective-permute-start | bytes 737288 | tf_op jit(solution)/shard_map/ppermute | solution.py:321
  80.2 4.5 %collective-permute-start.4 = (bf16[192,640]{1,0:T(8,128)(2,1)}, bf16[192,640]{1,0:T(8,128)(2,1)S(1)}, u32[]{:S(2)}, u32[]{:S(2)}) collective-permute-start(bf16[192,640]{1,0:T(8,128)(2,1)} %slice_bitcast_fusion), channel_id=1, source_target_pairs={{0,24},{8,0},{16,8},{24,16},{1,25},{9,1},{17,9},{25,17},{2,26},{10... | collective-permute-start | bytes 737288 | tf_op jit(solution)/shard_map/ppermute | solution.py:322
  85.8 2.3 %collective-permute-done.4.over_up = bf16[192,640]{1,0:T(8,128)(2,1)S(1)} collective-permute-done((bf16[192,640]{1,0:T(8,128)(2,1)}, bf16[192,640]{1,0:T(8,128)(2,1)S(1)}, u32[]{:S(2)}, u32[]{:S(2)}) %collective-permute-start.4) | collective-permute-done | bytes 245792 | tf_op jit(solution)/shard_map/ppermute | solution.py:322
  88.1 3.0 %shard_map.120 = (bf16[384,768]{1,0:T(8,128)(2,1)S(1)}, bf16[384,768]{1,0:T(8,128)(2,1)S(1)}) custom-call(s32[12]{0:T(128)S(1)} %concatenate.7.nums, bf16[2,192,640]{2,1,0:T(8,128)(2,1)S(1)} %bitcast.27, bf16[2,192,640]{2,1,0:T(8,128)(2,1)S(1)} %collective-permute-done.1.right, bf16[2,192,640]{2,1,0:T(8,128)(2,1)S(1)} %collective-permute-done.2.left, ...), custom_call_target="tpu_custom_call" | custom-call | flops 754974720 | bytes 4130096 | tf_op jit(solution)/shard_map/pallas_call | solution.py:27
  91.0 8.6 %collective-permute-start.5 = (bf16[384,768]{1,0:T(8,128)(2,1)S(1)}, bf16[384,768]{1,0:T(8,128)(2,1)S(1)}, u32[]{:S(2)}, u32[]{:S(2)}) collective-permute-start(bf16[384,768]{1,0:T(8,128)(2,1)S(1)} %get-tuple-element.19), channel_id=1, source_target_pairs={{0,1},{1,0},{2,3},{3,2},{4,5},{5,4},{6,7},{7,6},{8,9},{9,8},{10,11... | collective-permute-start | bytes 1769480 | tf_op jit(solution)/shard_map/ppermute | solution.py:338
  101.9 3.1 %collective-permute-start.6 = (bf16[96,768]{1,0:T(8,128)(2,1)S(1)}, bf16[96,768]{1,0:T(8,128)(2,1)S(1)}, u32[]{:S(2)}, u32[]{:S(2)}) collective-permute-start(bf16[96,768]{1,0:T(8,128)(2,1)S(1)} %get-tuple-element.21), channel_id=1, source_target_pairs={{0,2},{2,4},{4,6},{6,0},{1,3},{3,5},{5,7},{7,1},{8,10},{10,12},{12... | collective-permute-start | bytes 442376 | tf_op jit(solution)/shard_map/ppermute | solution.py:342
  105.0 4.6 %collective-permute-start.7 = (bf16[96,768]{1,0:T(8,128)(2,1)S(1)}, bf16[96,768]{1,0:T(8,128)(2,1)S(1)}, u32[]{:S(2)}, u32[]{:S(2)}) collective-permute-start(bf16[96,768]{1,0:T(8,128)(2,1)S(1)} %get-tuple-element.22), channel_id=1, source_target_pairs={{0,4},{2,6},{4,0},{6,2},{1,5},{3,7},{5,1},{7,3},{8,12},{10,14},{12... | collective-permute-start | bytes 442376 | tf_op jit(solution)/shard_map/ppermute | solution.py:342
  109.6 4.3 %collective-permute-start.8 = (bf16[96,768]{1,0:T(8,128)(2,1)S(1)}, bf16[96,768]{1,0:T(8,128)(2,1)S(1)}, u32[]{:S(2)}, u32[]{:S(2)}) collective-permute-start(bf16[96,768]{1,0:T(8,128)(2,1)S(1)} %get-tuple-element.23), channel_id=1, source_target_pairs={{0,6},{2,0},{4,2},{6,4},{1,7},{3,1},{5,3},{7,5},{8,14},{10,8},{12,... | collective-permute-start | bytes 442376 | tf_op jit(solution)/shard_map/ppermute | solution.py:342
  113.9 3.8 %collective-permute-done.7.refs_2_ = bf16[96,768]{1,0:T(8,128)(2,1)S(1)} collective-permute-done((bf16[96,768]{1,0:T(8,128)(2,1)S(1)}, bf16[96,768]{1,0:T(8,128)(2,1)S(1)}, u32[]{:S(2)}, u32[]{:S(2)}) %collective-permute-start.7) | collective-permute-done | bytes 147488 | tf_op jit(solution)/shard_map/ppermute | solution.py:342
  118.0 20.6 %all_gather.3.every = bf16[768,652]{1,0:T(8,128)(2,1)S(1)} all-gather(bf16[96,652]{1,0:T(8,128)(2,1)S(1)} %shard_map.122), channel_id=1, replica_groups=mesh['y'=8,'zh'=2,'x'=4,'zl'=4,'c'=2] {'zl','c'}, dimensions={0}, use_global_device_ids=true | all-gather | bytes 1126656 | tf_op jit(solution)/shard_map/all_gather | solution.py:348
  138.6 3.7 %shard_map.123 = (bf16[4,272,640]{2,1,0:T(8,128)(2,1)S(1)}, bf16[16,640]{1,0:T(8,128)(2,1)S(1)}) custom-call(s32[12]{0:T(128)S(1)} %concatenate.7.nums, bf16[2,192,640]{2,1,0:T(8,128)(2,1)S(1)} %bitcast.28, bf16[2,192,640]{2,1,0:T(8,128)(2,1)S(1)} %collective-permute-done.1.right, bf16[2,192,640]{2,1,0:T(8,128)(2,1)S(1)} %collective-permute-done.2.left, ...), custom_call_target="tpu_custom_call" | custom-call | flops 1258291200 | bytes 4934960 | tf_op jit(solution)/shard_map/pallas_call | solution.py:27
  142.3 22.5 %all_to_all.28.parts = bf16[4,272,640]{2,1,0:T(8,128)(2,1)S(1)} all-to-all(bf16[4,272,640]{2,1,0:T(8,128)(2,1)S(1)} %get-tuple-element.24), channel_id=1, replica_groups=mesh['y'=8,'zh'=2,'x'=4,'zl'=4,'c'=2] {'x'}, dimensions={0} | all-to-all | bytes 2785280 | tf_op jit(solution)/shard_map/all_to_all | solution.py:359
  165.8 7.9 %all-to-all-start.3 = ((bf16[16,16,768]{2,1,0:T(8,128)(2,1)}), bf16[16,16,768]{2,1,0:T(8,128)(2,1)S(1)}, u32[]{:S(2)}, u32[]{:S(2)}) async-start(bf16[16,16,768]{2,1,0:T(8,128)(2,1)} %shard_map.124), calls=%async_computation.3 | async-start | bytes 786432 | tf_op jit(solution)/shard_map/all_to_all | solution.py:363
  173.7 2.7 %shard_map.126 = (bf16[216,640]{1,0:T(8,128)(2,1)}, bf16[216,640]{1,0:T(8,128)(2,1)}, bf16[216,640]{1,0:T(8,128)(2,1)}) custom-call(bf16[2,192,640]{2,1,0:T(8,128)(2,1)S(1)} %bitcast.29, bf16[2,192,640]{2,1,0:T(8,128)(2,1)S(1)} %collective-permute-done.1.right, bf16[2,192,640]{2,1,0:T(8,128)(2,1)S(1)} %collective-permute-done.2.left, ...), custom_call_target="tpu_custom_call" | custom-call | flops 754974720 | bytes 3798272 | tf_op jit(solution)/shard_map/pallas_call | solution.py:27
  176.4 13.6 %all-to-all-done.3.parts = bf16[16,16,768]{2,1,0:T(8,128)(2,1)S(1)} async-done(((bf16[16,16,768]{2,1,0:T(8,128)(2,1)}), bf16[16,16,768]{2,1,0:T(8,128)(2,1)S(1)}, u32[]{:S(2)}, u32[]{:S(2)}) %all-to-all-start.3) | async-done | bytes 393248 | tf_op jit(solution)/shard_map/all_to_all | solution.py:363
  (58 shorter events, 14.7 us)
Async XLA Ops:
  0.6 1.0 copy-start
  1.6 1.0 copy-start.1
  3.2 12.5 %copy-start.12 = (s32[16]{0:T(128)S(1)}, s32[16]{0:T(128)}, u32[]{:S(2)}) copy-start(s32[16]{0:T(128)} %param.10) | copy-start | bytes 196
  3.2 12.7 %copy-start.9 = (s32[4]{0:T(128)S(1)}, s32[4]{0:T(128)}, u32[]{:S(2)}) copy-start(s32[4]{0:T(128)} %live.1) | copy-start | bytes 52
  5.2 29.2 %all-to-all-start = ((bf16[32,16,640]{2,1,0:T(8,128)(2,1)}), bf16[32,16,640]{2,1,0:T(8,128)(2,1)S(1)}, u32[]{:S(2)}, u32[]{:S(2)}) async-start(bf16[32,16,640]{2,1,0:T(8,128)(2,1)} %bitcast.5), calls=%async_computation | async-start | bytes 1310720 | tf_op jit(solution)/shard_map/all_to_all | solution.py:287
  34.5 12.3 %collective-permute-start = (bf16[48,640]{1,0:T(8,128)(2,1)S(1)}, bf16[48,640]{1,0:T(8,128)(2,1)S(1)}, u32[]{:S(2)}, u32[]{:S(2)}) collective-permute-start(bf16[48,640]{1,0:T(8,128)(2,1)S(1)} %bitcast.35), channel_id=1, source_target_pairs={{0,32},{32,0},{1,33},{33,1},{2,34},{34,2},{3,35},{35,3},{4,36},{36... | collective-permute-start | bytes 184328 | tf_op jit(solution)/shard_map/ppermute | solution.py:306
  47.7 16.2 %all-to-all-start.1 = ((bf16[8,48,640]{2,1,0:T(8,128)(2,1)}), bf16[8,48,640]{2,1,0:T(8,128)(2,1)S(1)}, u32[]{:S(2)}, u32[]{:S(2)}) async-start(bf16[8,48,640]{2,1,0:T(8,128)(2,1)} %broadcast_in_dim.55), calls=%async_computation.1 | async-start | bytes 983040 | tf_op jit(solution)/shard_map/all_to_all | solution.py:310
  63.9 20.8 %copy-start.11 = (bf16[640]{0:T(1024)(128)(2,1)S(1)}, bf16[640]{0:T(1024)(128)(2,1)}, u32[]{:S(2)}) copy-start(bf16[640]{0:T(1024)(128)(2,1)} %param.15) | copy-start | bytes 3844
  63.9 20.8 %copy-start.2 = (bf16[640,216]{0,1:T(8,128)(2,1)S(1)}, bf16[640,216]{0,1:T(8,128)(2,1)}, u32[]{:S(2)}) copy-start(bf16[640,216]{0,1:T(8,128)(2,1)} %param.12) | copy-start | bytes 829444
  64.9 19.8 %copy-start.4 = (bf16[640,216]{0,1:T(8,128)(2,1)S(1)}, bf16[640,216]{0,1:T(8,128)(2,1)}, u32[]{:S(2)}) copy-start(bf16[640,216]{0,1:T(8,128)(2,1)} %param.13) | copy-start | bytes 829444
  64.9 19.8 %copy-start.10 = (bf16[216,640]{1,0:T(8,128)(2,1)S(1)}, bf16[216,640]{1,0:T(8,128)(2,1)}, u32[]{:S(2)}) copy-start(bf16[216,640]{1,0:T(8,128)(2,1)} %param.14) | copy-start | bytes 829444
  64.9 11.7 %collective-permute-start.1 = (bf16[2,192,640]{2,1,0:T(8,128)(2,1)S(1)}, bf16[2,192,640]{2,1,0:T(8,128)(2,1)S(1)}, u32[]{:S(2)}, u32[]{:S(2)}) collective-permute-start(bf16[2,192,640]{2,1,0:T(8,128)(2,1)S(1)} %bitcast.25), channel_id=1, source_target_pairs={{0,8},{8,16},{16,24},{24,0},{1,9},{9,17},{17,25},{25,1},{2,10},{10... | collective-permute-start | bytes 1474568 | tf_op jit(solution)/shard_map/ppermute | solution.py:319
  68.5 10.9 %collective-permute-start.2 = (bf16[2,192,640]{2,1,0:T(8,128)(2,1)S(1)}, bf16[2,192,640]{2,1,0:T(8,128)(2,1)S(1)}, u32[]{:S(2)}, u32[]{:S(2)}) collective-permute-start(bf16[2,192,640]{2,1,0:T(8,128)(2,1)S(1)} %bitcast.26), channel_id=1, source_target_pairs={{0,24},{8,0},{16,8},{24,16},{1,25},{9,1},{17,9},{25,17},{2,26},{10... | collective-permute-start | bytes 1474568 | tf_op jit(solution)/shard_map/ppermute | solution.py:320
  77.4 8.3 %collective-permute-start.3 = (bf16[192,640]{1,0:T(8,128)(2,1)}, bf16[192,640]{1,0:T(8,128)(2,1)S(1)}, u32[]{:S(2)}, u32[]{:S(2)}) collective-permute-start(bf16[192,640]{1,0:T(8,128)(2,1)} %slice_bitcast_fusion.1), channel_id=1, source_target_pairs={{0,8},{8,16},{16,24},{24,0},{1,9},{9,17},{17,25},{25,1},{2,10},{10... | collective-permute-start | bytes 737288 | tf_op jit(solution)/shard_map/ppermute | solution.py:321
  80.2 7.9 %collective-permute-start.4 = (bf16[192,640]{1,0:T(8,128)(2,1)}, bf16[192,640]{1,0:T(8,128)(2,1)S(1)}, u32[]{:S(2)}, u32[]{:S(2)}) collective-permute-start(bf16[192,640]{1,0:T(8,128)(2,1)} %slice_bitcast_fusion), channel_id=1, source_target_pairs={{0,24},{8,0},{16,8},{24,16},{1,25},{9,1},{17,9},{25,17},{2,26},{10... | collective-permute-start | bytes 737288 | tf_op jit(solution)/shard_map/ppermute | solution.py:322
  91.0 10.2 %collective-permute-start.5 = (bf16[384,768]{1,0:T(8,128)(2,1)S(1)}, bf16[384,768]{1,0:T(8,128)(2,1)S(1)}, u32[]{:S(2)}, u32[]{:S(2)}) collective-permute-start(bf16[384,768]{1,0:T(8,128)(2,1)S(1)} %get-tuple-element.19), channel_id=1, source_target_pairs={{0,1},{1,0},{2,3},{3,2},{4,5},{5,4},{6,7},{7,6},{8,9},{9,8},{10,11... | collective-permute-start | bytes 1769480 | tf_op jit(solution)/shard_map/ppermute | solution.py:338
  101.2 37.4 %copy-start.3 = (bf16[640,216]{0,1:T(8,128)(2,1)S(1)}, bf16[640,216]{0,1:T(8,128)(2,1)}, u32[]{:S(2)}) copy-start(bf16[640,216]{0,1:T(8,128)(2,1)} %param.12) | copy-start | bytes 829444
  101.2 37.4 %copy-start.5 = (bf16[640,216]{0,1:T(8,128)(2,1)S(1)}, bf16[640,216]{0,1:T(8,128)(2,1)}, u32[]{:S(2)}) copy-start(bf16[640,216]{0,1:T(8,128)(2,1)} %param.13) | copy-start | bytes 829444
  101.9 12.0 %collective-permute-start.6 = (bf16[96,768]{1,0:T(8,128)(2,1)S(1)}, bf16[96,768]{1,0:T(8,128)(2,1)S(1)}, u32[]{:S(2)}, u32[]{:S(2)}) collective-permute-start(bf16[96,768]{1,0:T(8,128)(2,1)S(1)} %get-tuple-element.21), channel_id=1, source_target_pairs={{0,2},{2,4},{4,6},{6,0},{1,3},{3,5},{5,7},{7,1},{8,10},{10,12},{12... | collective-permute-start | bytes 442376 | tf_op jit(solution)/shard_map/ppermute | solution.py:342
  105.0 12.7 %collective-permute-start.7 = (bf16[96,768]{1,0:T(8,128)(2,1)S(1)}, bf16[96,768]{1,0:T(8,128)(2,1)S(1)}, u32[]{:S(2)}, u32[]{:S(2)}) collective-permute-start(bf16[96,768]{1,0:T(8,128)(2,1)S(1)} %get-tuple-element.22), channel_id=1, source_target_pairs={{0,4},{2,6},{4,0},{6,2},{1,5},{3,7},{5,1},{7,3},{8,12},{10,14},{12... | collective-permute-start | bytes 442376 | tf_op jit(solution)/shard_map/ppermute | solution.py:342
  109.6 8.0 %collective-permute-start.8 = (bf16[96,768]{1,0:T(8,128)(2,1)S(1)}, bf16[96,768]{1,0:T(8,128)(2,1)S(1)}, u32[]{:S(2)}, u32[]{:S(2)}) collective-permute-start(bf16[96,768]{1,0:T(8,128)(2,1)S(1)} %get-tuple-element.23), channel_id=1, source_target_pairs={{0,6},{2,0},{4,2},{6,4},{1,7},{3,1},{5,3},{7,5},{8,14},{10,8},{12,... | collective-permute-start | bytes 442376 | tf_op jit(solution)/shard_map/ppermute | solution.py:342
  142.3 22.6 %copy-start.6 = (bf16[16,640]{1,0:T(8,128)(2,1)}, bf16[16,640]{1,0:T(8,128)(2,1)S(1)}, u32[]{:S(2)}) copy-start(bf16[16,640]{1,0:T(8,128)(2,1)S(1)} %get-tuple-element.25.up_own) | copy-start | bytes 61444
  165.8 24.2 %all-to-all-start.3 = ((bf16[16,16,768]{2,1,0:T(8,128)(2,1)}), bf16[16,16,768]{2,1,0:T(8,128)(2,1)S(1)}, u32[]{:S(2)}, u32[]{:S(2)}) async-start(bf16[16,16,768]{2,1,0:T(8,128)(2,1)} %shard_map.124), calls=%async_computation.3 | async-start | bytes 786432 | tf_op jit(solution)/shard_map/all_to_all | solution.py:363
  190.0 0.7 copy-start.7
  (1 other events, 0.7 us)
where the time goes:
time: 194 us; the launch traced here: 192 us
  starting transfers between devices  66.6 us (34%)
  waiting for transfers between devices  59.2 us (31%)
  blocking collectives  43.1 us (22%)
  Pallas kernels  14 us (7%)
  local copies, waits for them, and re-layouts  5.81 us (3%)
    all_to_all x1, blocking collectives, per_device(): out = lax.all_to_all(out, 'x', 0, 0, tiled=True)  22.5 us
    all_gather x1, blocking collectives, per_device(): every = lax.all_gather(point, ('zl', 'c'), axis=0, tiled=True)  20.6 us
    all_to_all x1, waiting for transfers between devices, per_device(): lax.all_to_all(send, ('y', 'x'), 0, 0, tiled=True)  18.2 us
    pallas_call x8, Pallas kernels, call(): pl.pallas_call(body, out_shape=outs, in_specs=[SMEM if a.ndim == 1 else V...  14 us
    all_to_all x1, waiting for transfers between devices, per_device(): out = lax.all_to_all(out, ('y', 'zh'), 0, 0, tiled=True)  13.6 us
    all_to_all x1, waiting for transfers between devices, per_device(): column = lax.all_to_all(copies, 'y', 0, 0, tiled=True)  12.6 us
    ppermute x3, starting transfers between devices, per_device(): lax.ppermute(pairs[i], 'zl', [(a, (a + i) % nzl) for a in range(nzl)])  12 us
    ppermute x1, starting transfers between devices, per_device(): other = lax.ppermute(packed, 'zh', [(0, 1), (1, 0)])  10.7 us
  transfers between devices with their start and end apart: 12, of which 9 were waited for; matrix products, arithmetic and copies ran while one was open for 1% of the time, Pallas kernels for 1%

commit v1 on v0

--- a/solution.py
+++ b/solution.py
@@ -68,78 +68,113 @@
     send[...] = (contract(first, act[0], 1, 0) + contract(second, grad[0], 1, 0)).astype(BF16)
 
 
-def terms_kernel(hid, nums, own, right, left, over_in, over_up, gain, gate, up, down, keep, send):
+TAIL = 16
+
+
+def terms_kernel(nums, own, right, left, over_in, over_up, gain, ahead, behind, rest, keep, send):
     core = nums[CORE]
     gain_wide = gain[...].astype(F32)
+    n = over_in.shape[0]
+    chunk = n // 2
+    ones = jnp.ones(rest.shape, BF16)
     for k in range(4):
         inputs, upstream = pick((own, right, left, over_in, over_up), k)
-        n = inputs.shape[0]
         wide = inputs.astype(F32)
-        squares = jnp.sum(wide * wide, axis=1, keepdims=True)
-        sq_hi = squares.astype(BF16).astype(F32)
         scaled = (wide * gain_wide).astype(BF16)
-        lane = lax.broadcasted_iota(jnp.int32, (n, WIDE), 1)
-        first = contract(scaled, gate[...], 1, 1)
-        first = jnp.where(lane == hid, sq_hi, jnp.where(lane == hid + 1, squares - sq_hi, first))
-        parts = (
-            first.astype(BF16),
-            contract(scaled, up[...], 1, 1).astype(BF16),
-            contract(upstream, down[...], 1, 1).astype(BF16),
-        )
-        at = (k % 2) * n
+        main = contract(scaled, ahead[...], 1, 1) + contract(upstream, behind[...], 1, 1)
+        main = main.astype(BF16)
+        squares = wide * wide
+        high = squares.astype(BF16)
+        low = (squares - high.astype(F32)).astype(BF16)
+        tails = []
+        for h in range(2):
+            r = slice(h * chunk, (h + 1) * chunk)
+            total = contract(ones, high[r], 1, 1) + contract(ones, low[r], 1, 1)
+            total_hi = total.astype(BF16).astype(F32)
+            row = lax.broadcasted_iota(jnp.int32, total.shape, 0)
+            total = jnp.where(row == 0, total_hi, jnp.where(row == 1, total - total_hi, 0.0))
+            tails.append(jnp.concatenate([contract(rest[...], upstream[r], 1, 1), total], axis=0).astype(BF16))
 
         def store(out):
-            for i, part in enumerate(parts):
-                out[at : at + n, i * WIDE : (i + 1) * WIDE] = part
+            for h in range(2):
+                at = (k % 2) * 2 + h
+                for i in range(main.shape[1] // 128):
+                    out[at, i * chunk : (i + 1) * chunk, :] = main[
+                        h * chunk : (h + 1) * chunk, i * 128 : (i + 1) * 128
+                    ]
+                out[at, -TAIL:, :] = jnp.zeros((TAIL, 128), BF16)
+                out[at, -TAIL:, :chunk] = tails[h]
 
         pl.when(core == k // 2)(functools.partial(store, keep))
         pl.when(core != k // 2)(functools.partial(store, send))
 
 
 def pair_kernel(nums, keep, recv, *outs):
-    own = outs[0].shape[0]
     for i, out in enumerate(outs):
         chunk = (nums[LINE] + i) & (len(outs) - 1)
-        rows = pl.ds(pl.multiple_of(chunk * own, own), own)
-        out[...] = (keep[rows, :].astype(F32) + recv[rows, :].astype(F32)).astype(BF16)
+        out[...] = (keep[chunk].astype(F32) + recv[chunk].astype(F32)).astype(BF16)
 
 
 def point_kernel(hid, features, *refs):
-    terms, out = refs[:-1], refs[-1]
-
-    def total(i):
-        s = slice(i * WIDE, (i + 1) * WIDE)
-        return sum((t[:, s].astype(F32) for t in terms[1:]), terms[0][:, s].astype(F32))
-
-    gate, up, hidden_grad = total(0), total(1), total(2)
-    lane = lax.broadcasted_iota(jnp.int32, gate.shape, 1)
-    squares = jnp.sum(jnp.where((lane == hid) | (lane == hid + 1), gate, 0.0), axis=1, keepdims=True)
+    terms, (out, main_ref, hg_ref, tail_ref) = refs[:-4], refs[-4:]
+    rows, width = main_ref.shape
+    total = terms[0][...].astype(F32)
+    for t in terms[1:]:
+        total = total + t[...].astype(F32)
+    for i in range(width // 128):
+        main_ref[:, i * 128 : (i + 1) * 128] = total[i * rows : (i + 1) * rows]
+    tail = total[-TAIL:].T[:rows]
+    inside = width - 2 * hid
+    gate = main_ref[:, :hid]
+    up = main_ref[:, hid : 2 * hid]
+    hg_ref[:, :inside] = main_ref[:, 2 * hid :]
+    hg_ref[:, inside:] = tail[:, : hid - inside]
+    hidden_grad = hg_ref[...]
+    squares = tail[:, hid - inside : hid - inside + 1] + tail[:, hid - inside + 1 : hid - inside + 2]
     inv_rms = lax.rsqrt(squares / features + 1e-05)
-    gate = jnp.where(lane < hid, gate, 0.0) * inv_rms
+    gate = gate * inv_rms
     up = up * inv_rms
     logistic = jax.nn.sigmoid(gate)
     swished = gate * logistic
     slopes = logistic * (1.0 + gate * (1.0 - logistic))
-    hidden = swished * up
-    d_gate = (hidden_grad * up * slopes).astype(BF16)
-    d_up = (hidden_grad * swished).astype(BF16)
-    inner = jnp.sum(d_gate.astype(F32) * gate + d_up.astype(F32) * up, axis=1, keepdims=True)
-    lane = lax.broadcasted_iota(jnp.int32, (gate.shape[0], 4), 1)
+    d_gate = (hidden_grad * up * slopes).astype(BF16).astype(F32)
+    d_up = (hidden_grad * swished).astype(BF16).astype(F32)
+    inner = jnp.sum(d_gate * gate + d_up * up, axis=1, keepdims=True)
+    main_ref[:, :hid] = swished * up
+    main_ref[:, hid : 2 * hid] = d_gate
+    main_ref[:, 2 * hid :] = d_up[:, :inside]
     inv_hi = inv_rms.astype(BF16).astype(F32)
     in_hi = inner.astype(BF16).astype(F32)
-    tail = jnp.where(
-        lane == 0, inv_hi, jnp.where(lane == 1, inv_rms - inv_hi, jnp.where(lane == 2, in_hi, inner - in_hi))
-    )
-    out[:, :hid] = hidden[:, :hid].astype(BF16)
-    out[:, hid : 2 * hid] = d_gate[:, :hid]
-    out[:, 2 * hid : 3 * hid] = d_up[:, :hid]
-    out[:, 3 * hid :] = tail.astype(BF16)
-
-
-def rows_of(every, k, n):
-    cores, own = 2, n // 2
-    at = [(((k % 2) * 2 + j) * cores + k // 2) * own for j in range(2)]
-    return jnp.concatenate([every[a : a + own, :] for a in at], axis=0)
+    tail_ref[...] = jnp.zeros(tail_ref.shape, F32)
+    tail_ref[:rows, : hid - inside] = d_up[:, inside:]
+    for i, v in enumerate((inv_hi, inv_rms - inv_hi, in_hi, inner - in_hi)):
+        at = hid - inside + i
+        tail_ref[:rows, at : at + 1] = v
+    for i in range(width // 128):
+        out[i * rows : (i + 1) * rows, :] = main_ref[:, i * 128 : (i + 1) * 128].astype(BF16)
+    out[-TAIL:, :] = tail_ref[...].T[:TAIL].astype(BF16)
+
+
+def rows_of(every, k, n, hid, width, pay_ref):
+    own = n // 2
+    pieces = width // 128
+    size = pieces * own + TAIL
+    inside = width - 2 * hid
+    tails = []
+    for j in range(2):
+        at = (((k % 2) * 2 + j) * 2 + k // 2) * size
+        r = slice(k * n + j * own, k * n + (j + 1) * own)
+        main = jnp.concatenate(
+            [every[at + i * own : at + (i + 1) * own, :] for i in range(pieces)], axis=1
+        )
+        tail = every[at + pieces * own : at + size, :].astype(F32).T[:own]
+        pay_ref[0, r, :hid] = main[:, :hid]
+        pay_ref[1, r, :hid] = main[:, hid : 2 * hid]
+        pay_ref[2, r, :inside] = main[:, 2 * hid :]
+        pay_ref[2, r, inside:hid] = tail[:, : hid - inside].astype(BF16)
+        tails.append(tail[:, hid - inside :])
+    tail = jnp.concatenate(tails, axis=0)
+    return tail[:, 0:1] + tail[:, 1:2], tail[:, 2:3] + tail[:, 3:4]
 
 
 def where_packed(nums, row, batches, tokens, per, nx, block, part):
@@ -159,7 +194,7 @@
 
 def term_kernel(
     hid, features, plan, nums, own, right, left, over_in, over_up, every, gain, gate, up,
-    out, up_own, term_ref,
+    out, up_own, term_ref, pay_ref,
 ):
     nx = out.shape[0]
     gain_wide = gain[...].astype(F32)
@@ -171,17 +206,15 @@
     for k in range(4):
         inputs, upstream = pick((own, right, left, over_in, over_up), k)
         n = inputs.shape[0]
-        pay = rows_of(every, k, n)
-        tail = pay[:, 3 * hid :].astype(F32)
-        inv_rms = tail[:, 0:1] + tail[:, 1:2]
-        inner = tail[:, 2:3] + tail[:, 3:4]
-        d_normed = contract(pay[:, hid : 2 * hid], gate[...], 1, 0) + contract(
-            pay[:, 2 * hid : 3 * hid], up[...], 1, 0
+        s = slice(k * n, (k + 1) * n)
+        inv_rms, inner = rows_of(every, k, n, hid, inputs.shape[1], pay_ref)
+        d_normed = contract(pay_ref[1, s, :hid], gate[...], 1, 0) + contract(
+            pay_ref[2, s, :hid], up[...], 1, 0
         )
         unit = inputs.astype(F32) * inv_rms
         gain_term = gain_term + jnp.sum(d_normed * unit, axis=0, keepdims=True)
         term = inv_rms * (gain_wide * d_normed - unit * (inner / features))
-        term_ref[k * n : (k + 1) * n, :] = term.astype(BF16)
+        term_ref[s, :] = term.astype(BF16)
         column = lax.broadcasted_iota(jnp.int32, (own_rows, n), 1) + k * n
         hot = jnp.where(index == column, 1.0, 0.0).astype(BF16)
         own_total = own_total + contract(hot, upstream, 1, 0)
@@ -210,11 +243,7 @@
         inputs, upstream = pick((own, right, left, over_in, over_up), k)
         n = inputs.shape[0]
         s = slice(k * n, (k + 1) * n)
-        pay = rows_of(every, k, n)
-        tail = pay[:, 3 * hid :].astype(F32)
-        inv_rms = tail[:, 0:1] + tail[:, 1:2]
-        for i in range(3):
-            pay_ref[i, s, :hid] = pay[:, i * hid : (i + 1) * hid]
+        inv_rms, _ = rows_of(every, k, n, hid, inputs.shape[1], pay_ref)
         normed_ref[s, :] = (inputs.astype(F32) * inv_rms * gain_wide).astype(BF16)
         up_ref[s, :] = upstream
     grad_down[...] = contract(pay_ref[0, :, :hid], up_ref[...], 0, 0).astype(BF16)
@@ -314,36 +343,42 @@
     at = out_row % part
     hot = (at // block * 2 + out_row // part) * block + at % block == from_row
     own = contract(hot.astype(BF16), column, 1, 0).astype(BF16).reshape(2, part, width)
-    ahead = [(i, (i + 1) % nx) for i in range(nx)]
+    forth = [(i, (i + 1) % nx) for i in range(nx)]
     back = [(i, (i - 1) % nx) for i in range(nx)]
-    right = lax.ppermute(own, "x", ahead)
+    right = lax.ppermute(own, "x", forth)
     left = lax.ppermute(own, "x", back)
-    over_in = lax.ppermute(right[0], "x", ahead)
+    over_in = lax.ppermute(right[0], "x", forth)
     over_up = lax.ppermute(left[1], "x", back)
     blocks = (own, right, left, over_in, over_up)
 
-    pad = ((0, WIDE - hid), (0, 0))
+    inside = width - 2 * hid
     gate_rows, up_rows = gate_weight.T, up_weight.T
-    gate_pad, up_pad, down_pad = (jnp.pad(w, pad) for w in (gate_rows, up_rows, down_weight))
+    ahead_rows = jnp.concatenate([gate_rows, up_rows, jnp.zeros((inside, width), BF16)], axis=0)
+    behind_rows = jnp.concatenate([jnp.zeros((2 * hid, width), BF16), down_weight[:inside]], axis=0)
+    rest_rows = down_weight[inside:]
     gain = norm_gain.reshape(1, width)
-    lanes = 3 * WIDE
-    half = live // nc
-    own_count = half // nzl
-
+    own_count = live // nc // nzl
+    size = own_count * (width // 128) + TAIL
     product = 2 * live * width * WIDE
+    halves = shape(nzl, size, 128)
     keep, give = call(
-        functools.partial(terms_kernel, hid), (shape(half, lanes), shape(half, lanes)), [], 3 * product,
-        nums, *blocks, gain, gate_pad, up_pad, down_pad,
+        terms_kernel, (halves, halves), [], 5 * product,
+        nums, *blocks, gain, ahead_rows, behind_rows, rest_rows,
     )
     taken = lax.ppermute(give, "c", [(0, 1), (1, 0)])
-    chunk = shape(own_count, lanes)
-    pairs = call(pair_kernel, (chunk,) * nzl, [], half * lanes, nums, keep, taken)
+    chunk = shape(size, 128)
+    pairs = call(pair_kernel, (chunk,) * nzl, [], nzl * size * 128, nums, keep, taken)
     others = [
         lax.ppermute(pairs[i], "zl", [(a, (a + i) % nzl) for a in range(nzl)]) for i in range(1, nzl)
     ]
     point = call(
-        functools.partial(point_kernel, hid, features), shape(own_count, 3 * hid + 4), [],
-        20 * own_count * lanes, pairs[0], *others,
+        functools.partial(point_kernel, hid, features), chunk,
+        [
+            pltpu.VMEM((own_count, width), F32),
+            pltpu.VMEM((own_count, hid), F32),
+            pltpu.VMEM((128, 128), F32),
+        ],
+        20 * size * 128, pairs[0], *others,
     )
     every = lax.all_gather(point, ("zl", "c"), axis=0, tiled=True)
 
@@ -352,7 +387,7 @@
     out, up_own = call(
         functools.partial(term_kernel, hid, features, plan),
         (shape(nx, count + 16, width), shape(own_rows, width)),
-        [pltpu.VMEM((live, width), BF16)],
+        [pltpu.VMEM((live, width), BF16), pltpu.VMEM((3, live, WIDE), BF16)],
         5 * product,
         nums, *blocks, every, gain, gate_rows, up_rows,
     )

time: 194 us -> 194 us (level)
  waiting for transfers between devices: 59.2 us -> 55.8 us
  transfers between devices with their start and end apart: 12 -> 12, of which waited for: 9 -> 8; matrix products, arithmetic and copies ran while one was open for 1% -> 2% of each run, Pallas kernels for 1% -> 1%
where the time goes in v1:
time: 194 us; the launch traced here: 192 us
  starting transfers between devices  68.5 us (35%)
  waiting for transfers between devices  55.8 us (29%)
  blocking collectives  42 us (22%)
  Pallas kernels  15.8 us (8%)
  local copies, waits for them, and re-layouts  6.83 us (4%)
    all_to_all x1, blocking collectives, per_device(): out = lax.all_to_all(out, 'x', 0, 0, tiled=True)  22.5 us
    all_gather x1, blocking collectives, per_device(): every = lax.all_gather(point, ('zl', 'c'), axis=0, tiled=True)  19.5 us
    all_to_all x1, waiting for transfers between devices, per_device(): lax.all_to_all(send, ('y', 'x'), 0, 0, tiled=True)  18.2 us
    pallas_call x8, Pallas kernels, call(): pl.pallas_call(body, out_shape=outs, in_specs=[SMEM if a.ndim == 1 else V...  15.8 us
    all_to_all x1, waiting for transfers between devices, per_device(): out = lax.all_to_all(out, ('y', 'zh'), 0, 0, tiled=True)  13.6 us
    all_to_all x1, waiting for transfers between devices, per_device(): column = lax.all_to_all(copies, 'y', 0, 0, tiled=True)  12.6 us
    ppermute x3, starting transfers between devices, per_device(): lax.ppermute(pairs[i], 'zl', [(a, (a + i) % nzl) for a in range(nzl)])  12 us
    ppermute x1, starting transfers between devices, per_device(): other = lax.ppermute(packed, 'zh', [(0, 1), (1, 0)])  10.7 us
  transfers between devices with their start and end apart: 12, of which 8 were waited for; matrix products, arithmetic and copies ran while one was open for 2% of the time, Pallas kernels for 1%

profile of v1, /device:TPU:1, one launch (start us, length us, event | category | flops | bytes accessed | tf_op | source)
XLA Modules:
  0.0 192.4 jit_solution(3816783027020284413)
XLA Ops:
  3.2 2.0 %shard_map.119 = bf16[512,640]{1,0:T(8,128)(2,1)} custom-call(s32[4]{0:T(128)S(1)} %copy-done.9, bf16[1,256,640]{2,1,0:T(8,128)(2,1)S(1)} %copy-done, bf16[1,256,640]{2,1,0:T(8,128)(2,1)S(1)} %copy-done.1), custom_call_target="tpu_custom_call" | custom-call | flops 167772160 | bytes 1310736 | tf_op jit(solution)/shard_map/pallas_call | solution.py:27
  5.2 10.5 %all-to-all-start = ((bf16[32,16,640]{2,1,0:T(8,128)(2,1)}), bf16[32,16,640]{2,1,0:T(8,128)(2,1)S(1)}, u32[]{:S(2)}, u32[]{:S(2)}) async-start(bf16[32,16,640]{2,1,0:T(8,128)(2,1)} %bitcast.5), calls=%async_computation | async-start | bytes 1310720 | tf_op jit(solution)/shard_map/all_to_all | solution.py:316
  16.2 18.2 %all-to-all-done = bf16[32,16,640]{2,1,0:T(8,128)(2,1)S(1)} async-done(((bf16[32,16,640]{2,1,0:T(8,128)(2,1)}), bf16[32,16,640]{2,1,0:T(8,128)(2,1)S(1)}, u32[]{:S(2)}, u32[]{:S(2)}) %all-to-all-start) | async-done | bytes 655392 | tf_op jit(solution)/shard_map/all_to_all | solution.py:316
  34.5 10.7 %collective-permute-start = (bf16[48,640]{1,0:T(8,128)(2,1)S(1)}, bf16[48,640]{1,0:T(8,128)(2,1)S(1)}, u32[]{:S(2)}, u32[]{:S(2)}) collective-permute-start(bf16[48,640]{1,0:T(8,128)(2,1)S(1)} %bitcast.35), channel_id=1, source_target_pairs={{0,32},{32,0},{1,33},{33,1},{2,34},{34,2},{3,35},{35,3},{4,36},{36... | collective-permute-start | bytes 184328 | tf_op jit(solution)/shard_map/ppermute | solution.py:335
  47.7 3.5 %all-to-all-start.1 = ((bf16[8,48,640]{2,1,0:T(8,128)(2,1)}), bf16[8,48,640]{2,1,0:T(8,128)(2,1)S(1)}, u32[]{:S(2)}, u32[]{:S(2)}) async-start(bf16[8,48,640]{2,1,0:T(8,128)(2,1)} %broadcast_in_dim.59), calls=%async_computation.1 | async-start | bytes 983040 | tf_op jit(solution)/shard_map/all_to_all | solution.py:339
  51.2 12.6 %all-to-all-done.1 = bf16[8,48,640]{2,1,0:T(8,128)(2,1)S(1)} async-done(((bf16[8,48,640]{2,1,0:T(8,128)(2,1)}), bf16[8,48,640]{2,1,0:T(8,128)(2,1)S(1)}, u32[]{:S(2)}, u32[]{:S(2)}) %all-to-all-start.1) | async-done | bytes 491552 | tf_op jit(solution)/shard_map/all_to_all | solution.py:339
  64.9 3.5 %collective-permute-start.1 = (bf16[2,192,640]{2,1,0:T(8,128)(2,1)S(1)}, bf16[2,192,640]{2,1,0:T(8,128)(2,1)S(1)}, u32[]{:S(2)}, u32[]{:S(2)}) collective-permute-start(bf16[2,192,640]{2,1,0:T(8,128)(2,1)S(1)} %bitcast.25), channel_id=1, source_target_pairs={{0,8},{8,16},{16,24},{24,0},{1,9},{9,17},{17,25},{25,1},{2,10},{10... | collective-permute-start | bytes 1474568 | tf_op jit(solution)/shard_map/ppermute | solution.py:348
  68.5 3.5 %collective-permute-start.2 = (bf16[2,192,640]{2,1,0:T(8,128)(2,1)S(1)}, bf16[2,192,640]{2,1,0:T(8,128)(2,1)S(1)}, u32[]{:S(2)}, u32[]{:S(2)}) collective-permute-start(bf16[2,192,640]{2,1,0:T(8,128)(2,1)S(1)} %bitcast.26), channel_id=1, source_target_pairs={{0,24},{8,0},{16,8},{24,16},{1,25},{9,1},{17,9},{25,17},{2,26},{10... | collective-permute-start | bytes 1474568 | tf_op jit(solution)/shard_map/ppermute | solution.py:349
  72.7 4.0 %collective-permute-done.1.right = bf16[2,192,640]{2,1,0:T(8,128)(2,1)S(1)} collective-permute-done((bf16[2,192,640]{2,1,0:T(8,128)(2,1)S(1)}, bf16[2,192,640]{2,1,0:T(8,128)(2,1)S(1)}, u32[]{:S(2)}, u32[]{:S(2)}) %collective-permute-start.1) | collective-permute-done | bytes 491552 | tf_op jit(solution)/shard_map/ppermute | solution.py:348
  77.4 2.0 %collective-permute-start.3 = (bf16[192,640]{1,0:T(8,128)(2,1)}, bf16[192,640]{1,0:T(8,128)(2,1)S(1)}, u32[]{:S(2)}, u32[]{:S(2)}) collective-permute-start(bf16[192,640]{1,0:T(8,128)(2,1)} %slice_bitcast_fusion.1), channel_id=1, source_target_pairs={{0,8},{8,16},{16,24},{24,0},{1,9},{9,17},{17,25},{25,1},{2,10},{10... | collective-permute-start | bytes 737288 | tf_op jit(solution)/shard_map/ppermute | solution.py:350
  80.2 4.4 %collective-permute-start.4 = (bf16[192,640]{1,0:T(8,128)(2,1)}, bf16[192,640]{1,0:T(8,128)(2,1)S(1)}, u32[]{:S(2)}, u32[]{:S(2)}) collective-permute-start(bf16[192,640]{1,0:T(8,128)(2,1)} %slice_bitcast_fusion), channel_id=1, source_target_pairs={{0,24},{8,0},{16,8},{24,16},{1,25},{9,1},{17,9},{25,17},{2,26},{10... | collective-permute-start | bytes 737288 | tf_op jit(solution)/shard_map/ppermute | solution.py:351
  86.1 2.0 %collective-permute-done.4.over_up = bf16[192,640]{1,0:T(8,128)(2,1)S(1)} collective-permute-done((bf16[192,640]{1,0:T(8,128)(2,1)}, bf16[192,640]{1,0:T(8,128)(2,1)S(1)}, u32[]{:S(2)}, u32[]{:S(2)}) %collective-permute-start.4) | collective-permute-done | bytes 245792 | tf_op jit(solution)/shard_map/ppermute | solution.py:351
  88.1 4.5 %shard_map.120 = (bf16[4,496,128]{2,1,0:T(8,128)(2,1)S(1)}, bf16[4,496,128]{2,1,0:T(8,128)(2,1)S(1)}) custom-call(s32[12]{0:T(128)S(1)} %concatenate.13.nums, bf16[2,192,640]{2,1,0:T(8,128)(2,1)S(1)} %bitcast.27, bf16[2,192,640]{2,1,0:T(8,128)(2,1)S(1)} %collective-permute-done.1.right, bf16[2,192,640]{2,1,0:T(8,128)(2,1)S(1)} %collective-permute-done.2.left, ...), custom_call_target="tpu_custom_call" | custom-call | flops 1258291200 | bytes 4631856 | tf_op jit(solution)/shard_map/pallas_call | solution.py:27
  92.6 8.6 %collective-permute-start.5 = (bf16[4,496,128]{2,1,0:T(8,128)(2,1)S(1)}, bf16[4,496,128]{2,1,0:T(8,128)(2,1)S(1)}, u32[]{:S(2)}, u32[]{:S(2)}) collective-permute-start(bf16[4,496,128]{2,1,0:T(8,128)(2,1)S(1)} %get-tuple-element.19), channel_id=1, source_target_pairs={{0,1},{1,0},{2,3},{3,2},{4,5},{5,4},{6,7},{7,6},{8,9},{9,8},{10,11... | collective-permute-start | bytes 1523720 | tf_op jit(solution)/shard_map/ppermute | solution.py:368
  103.3 3.1 %collective-permute-start.6 = (bf16[496,128]{1,0:T(8,128)(2,1)S(1)}, bf16[496,128]{1,0:T(8,128)(2,1)S(1)}, u32[]{:S(2)}, u32[]{:S(2)}) collective-permute-start(bf16[496,128]{1,0:T(8,128)(2,1)S(1)} %get-tuple-element.21), channel_id=1, source_target_pairs={{0,2},{2,4},{4,6},{6,0},{1,3},{3,5},{5,7},{7,1},{8,10},{10,12},{12... | collective-permute-start | bytes 380936 | tf_op jit(solution)/shard_map/ppermute | solution.py:372
  106.4 4.6 %collective-permute-start.7 = (bf16[496,128]{1,0:T(8,128)(2,1)S(1)}, bf16[496,128]{1,0:T(8,128)(2,1)S(1)}, u32[]{:S(2)}, u32[]{:S(2)}) collective-permute-start(bf16[496,128]{1,0:T(8,128)(2,1)S(1)} %get-tuple-element.22), channel_id=1, source_target_pairs={{0,4},{2,6},{4,0},{6,2},{1,5},{3,7},{5,1},{7,3},{8,12},{10,14},{12... | collective-permute-start | bytes 380936 | tf_op jit(solution)/shard_map/ppermute | solution.py:372
  111.0 4.3 %collective-permute-start.8 = (bf16[496,128]{1,0:T(8,128)(2,1)S(1)}, bf16[496,128]{1,0:T(8,128)(2,1)S(1)}, u32[]{:S(2)}, u32[]{:S(2)}) collective-permute-start(bf16[496,128]{1,0:T(8,128)(2,1)S(1)} %get-tuple-element.23), channel_id=1, source_target_pairs={{0,6},{2,0},{4,2},{6,4},{1,7},{3,1},{5,3},{7,5},{8,14},{10,8},{12,... | collective-permute-start | bytes 380936 | tf_op jit(solution)/shard_map/ppermute | solution.py:372
  115.3 2.2 %collective-permute-done.8.refs_3_ = bf16[496,128]{1,0:T(8,128)(2,1)S(1)} collective-permute-done((bf16[496,128]{1,0:T(8,128)(2,1)S(1)}, bf16[496,128]{1,0:T(8,128)(2,1)S(1)}, u32[]{:S(2)}, u32[]{:S(2)}) %collective-permute-start.8) | collective-permute-done | bytes 127008 | tf_op jit(solution)/shard_map/ppermute | solution.py:372
  118.1 19.5 %all_gather.3.every = bf16[3968,128]{1,0:T(8,128)(2,1)S(1)} all-gather(bf16[496,128]{1,0:T(8,128)(2,1)S(1)} %shard_map.122), channel_id=1, replica_groups=mesh['y'=8,'zh'=2,'x'=4,'zl'=4,'c'=2] {'zl','c'}, dimensions={0}, use_global_device_ids=true | all-gather | bytes 1142784 | tf_op jit(solution)/shard_map/all_gather | solution.py:383
  137.6 4.0 %shard_map.123 = (bf16[4,272,640]{2,1,0:T(8,128)(2,1)S(1)}, bf16[16,640]{1,0:T(8,128)(2,1)S(1)}) custom-call(s32[12]{0:T(128)S(1)} %concatenate.13.nums, bf16[2,192,640]{2,1,0:T(8,128)(2,1)S(1)} %bitcast.28, bf16[2,192,640]{2,1,0:T(8,128)(2,1)S(1)} %collective-permute-done.1.right, bf16[2,192,640]{2,1,0:T(8,128)(2,1)S(1)} %collective-permute-done.2.left, ...), custom_call_target="tpu_custom_call" | custom-call | flops 1258291200 | bytes 4949296 | tf_op jit(solution)/shard_map/pallas_call | solution.py:27
  141.6 22.5 %all_to_all.28.parts = bf16[4,272,640]{2,1,0:T(8,128)(2,1)S(1)} all-to-all(bf16[4,272,640]{2,1,0:T(8,128)(2,1)S(1)} %get-tuple-element.24), channel_id=1, replica_groups=mesh['y'=8,'zh'=2,'x'=4,'zl'=4,'c'=2] {'x'}, dimensions={0} | all-to-all | bytes 2785280 | tf_op jit(solution)/shard_map/all_to_all | solution.py:394
  165.0 9.8 %all-to-all-start.3 = ((bf16[16,16,768]{2,1,0:T(8,128)(2,1)}), bf16[16,16,768]{2,1,0:T(8,128)(2,1)S(1)}, u32[]{:S(2)}, u32[]{:S(2)}) async-start(bf16[16,16,768]{2,1,0:T(8,128)(2,1)} %shard_map.124), calls=%async_computation.3 | async-start | bytes 786432 | tf_op jit(solution)/shard_map/all_to_all | solution.py:398
  174.8 2.6 %shard_map.126 = (bf16[216,640]{1,0:T(8,128)(2,1)}, bf16[216,640]{1,0:T(8,128)(2,1)}, bf16[216,640]{1,0:T(8,128)(2,1)}) custom-call(bf16[2,192,640]{2,1,0:T(8,128)(2,1)S(1)} %bitcast.29, bf16[2,192,640]{2,1,0:T(8,128)(2,1)S(1)} %collective-permute-done.1.right, bf16[2,192,640]{2,1,0:T(8,128)(2,1)S(1)} %collective-permute-done.2.left, ...), custom_call_target="tpu_custom_call" | custom-call | flops 754974720 | bytes 3812608 | tf_op jit(solution)/shard_map/pallas_call | solution.py:27
  177.5 13.6 %all-to-all-done.3.parts = bf16[16,16,768]{2,1,0:T(8,128)(2,1)S(1)} async-done(((bf16[16,16,768]{2,1,0:T(8,128)(2,1)}), bf16[16,16,768]{2,1,0:T(8,128)(2,1)S(1)}, u32[]{:S(2)}, u32[]{:S(2)}) %all-to-all-start.3) | async-done | bytes 393248 | tf_op jit(solution)/shard_map/all_to_all | solution.py:398
  (63 shorter events, 15.0 us)
Async XLA Ops:
  0.6 1.0 copy-start
  3.2 12.5 %copy-start.13 = (s32[16]{0:T(128)S(1)}, s32[16]{0:T(128)}, u32[]{:S(2)}) copy-start(s32[16]{0:T(128)} %param.10) | copy-start | bytes 196
  3.2 12.7 %copy-start.10 = (s32[4]{0:T(128)S(1)}, s32[4]{0:T(128)}, u32[]{:S(2)}) copy-start(s32[4]{0:T(128)} %live.1) | copy-start | bytes 52
  5.2 29.2 %all-to-all-start = ((bf16[32,16,640]{2,1,0:T(8,128)(2,1)}), bf16[32,16,640]{2,1,0:T(8,128)(2,1)S(1)}, u32[]{:S(2)}, u32[]{:S(2)}) async-start(bf16[32,16,640]{2,1,0:T(8,128)(2,1)} %bitcast.5), calls=%async_computation | async-start | bytes 1310720 | tf_op jit(solution)/shard_map/all_to_all | solution.py:316
  34.5 12.3 %collective-permute-start = (bf16[48,640]{1,0:T(8,128)(2,1)S(1)}, bf16[48,640]{1,0:T(8,128)(2,1)S(1)}, u32[]{:S(2)}, u32[]{:S(2)}) collective-permute-start(bf16[48,640]{1,0:T(8,128)(2,1)S(1)} %bitcast.35), channel_id=1, source_target_pairs={{0,32},{32,0},{1,33},{33,1},{2,34},{34,2},{3,35},{35,3},{4,36},{36... | collective-permute-start | bytes 184328 | tf_op jit(solution)/shard_map/ppermute | solution.py:335
  47.7 16.2 %all-to-all-start.1 = ((bf16[8,48,640]{2,1,0:T(8,128)(2,1)}), bf16[8,48,640]{2,1,0:T(8,128)(2,1)S(1)}, u32[]{:S(2)}, u32[]{:S(2)}) async-start(bf16[8,48,640]{2,1,0:T(8,128)(2,1)} %broadcast_in_dim.59), calls=%async_computation.1 | async-start | bytes 983040 | tf_op jit(solution)/shard_map/all_to_all | solution.py:339
  63.9 8.1 %copy-start.11 = (bf16[216,640]{1,0:T(8,128)(2,1)S(1)}, bf16[216,640]{1,0:T(8,128)(2,1)}, u32[]{:S(2)}) copy-start(bf16[216,640]{1,0:T(8,128)(2,1)} %param.14) | copy-start | bytes 829444
  64.9 19.7 %copy-start.12 = (bf16[640]{0:T(1024)(128)(2,1)S(1)}, bf16[640]{0:T(1024)(128)(2,1)}, u32[]{:S(2)}) copy-start(bf16[640]{0:T(1024)(128)(2,1)} %param.15) | copy-start | bytes 3844
  64.9 20.9 %copy-start.2 = (bf16[640,216]{0,1:T(8,128)(2,1)S(1)}, bf16[640,216]{0,1:T(8,128)(2,1)}, u32[]{:S(2)}) copy-start(bf16[640,216]{0,1:T(8,128)(2,1)} %param.13) | copy-start | bytes 829444
  64.9 20.9 %copy-start.3 = (bf16[640,216]{0,1:T(8,128)(2,1)S(1)}, bf16[640,216]{0,1:T(8,128)(2,1)}, u32[]{:S(2)}) copy-start(bf16[640,216]{0,1:T(8,128)(2,1)} %param.12) | copy-start | bytes 829444
  64.9 11.7 %collective-permute-start.1 = (bf16[2,192,640]{2,1,0:T(8,128)(2,1)S(1)}, bf16[2,192,640]{2,1,0:T(8,128)(2,1)S(1)}, u32[]{:S(2)}, u32[]{:S(2)}) collective-permute-start(bf16[2,192,640]{2,1,0:T(8,128)(2,1)S(1)} %bitcast.25), channel_id=1, source_target_pairs={{0,8},{8,16},{16,24},{24,0},{1,9},{9,17},{17,25},{25,1},{2,10},{10... | collective-permute-start | bytes 1474568 | tf_op jit(solution)/shard_map/ppermute | solution.py:348
  68.5 10.9 %collective-permute-start.2 = (bf16[2,192,640]{2,1,0:T(8,128)(2,1)S(1)}, bf16[2,192,640]{2,1,0:T(8,128)(2,1)S(1)}, u32[]{:S(2)}, u32[]{:S(2)}) collective-permute-start(bf16[2,192,640]{2,1,0:T(8,128)(2,1)S(1)} %bitcast.26), channel_id=1, source_target_pairs={{0,24},{8,0},{16,8},{24,16},{1,25},{9,1},{17,9},{25,17},{2,26},{10... | collective-permute-start | bytes 1474568 | tf_op jit(solution)/shard_map/ppermute | solution.py:349
  77.4 8.6 %collective-permute-start.3 = (bf16[192,640]{1,0:T(8,128)(2,1)}, bf16[192,640]{1,0:T(8,128)(2,1)S(1)}, u32[]{:S(2)}, u32[]{:S(2)}) collective-permute-start(bf16[192,640]{1,0:T(8,128)(2,1)} %slice_bitcast_fusion.1), channel_id=1, source_target_pairs={{0,8},{8,16},{16,24},{24,0},{1,9},{9,17},{17,25},{25,1},{2,10},{10... | collective-permute-start | bytes 737288 | tf_op jit(solution)/shard_map/ppermute | solution.py:350
  80.2 7.9 %collective-permute-start.4 = (bf16[192,640]{1,0:T(8,128)(2,1)}, bf16[192,640]{1,0:T(8,128)(2,1)S(1)}, u32[]{:S(2)}, u32[]{:S(2)}) collective-permute-start(bf16[192,640]{1,0:T(8,128)(2,1)} %slice_bitcast_fusion), channel_id=1, source_target_pairs={{0,24},{8,0},{16,8},{24,16},{1,25},{9,1},{17,9},{25,17},{2,26},{10... | collective-permute-start | bytes 737288 | tf_op jit(solution)/shard_map/ppermute | solution.py:351
  86.0 51.5 %copy-start.4 = (bf16[192,640]{1,0:T(8,128)(2,1)}, bf16[192,640]{1,0:T(8,128)(2,1)S(1)}, u32[]{:S(2)}) copy-start(bf16[192,640]{1,0:T(8,128)(2,1)S(1)} %collective-permute-done.3.over_in) | copy-start | bytes 737284
  88.1 4.5 %copy-start.6 = (bf16[192,640]{1,0:T(8,128)(2,1)}, bf16[192,640]{1,0:T(8,128)(2,1)S(1)}, u32[]{:S(2)}) copy-start(bf16[192,640]{1,0:T(8,128)(2,1)S(1)} %collective-permute-done.4.over_up) | copy-start | bytes 737284
  92.6 10.1 %collective-permute-start.5 = (bf16[4,496,128]{2,1,0:T(8,128)(2,1)S(1)}, bf16[4,496,128]{2,1,0:T(8,128)(2,1)S(1)}, u32[]{:S(2)}, u32[]{:S(2)}) collective-permute-start(bf16[4,496,128]{2,1,0:T(8,128)(2,1)S(1)} %get-tuple-element.19), channel_id=1, source_target_pairs={{0,1},{1,0},{2,3},{3,2},{4,5},{5,4},{6,7},{7,6},{8,9},{9,8},{10,11... | collective-permute-start | bytes 1523720 | tf_op jit(solution)/shard_map/ppermute | solution.py:368
  102.6 34.9 %copy-start.7 = (bf16[192,640]{1,0:T(8,128)(2,1)S(1)}, bf16[192,640]{1,0:T(8,128)(2,1)}, u32[]{:S(2)}) copy-start(bf16[192,640]{1,0:T(8,128)(2,1)} %copy-done.6) | copy-start | bytes 737284
  103.3 12.0 %collective-permute-start.6 = (bf16[496,128]{1,0:T(8,128)(2,1)S(1)}, bf16[496,128]{1,0:T(8,128)(2,1)S(1)}, u32[]{:S(2)}, u32[]{:S(2)}) collective-permute-start(bf16[496,128]{1,0:T(8,128)(2,1)S(1)} %get-tuple-element.21), channel_id=1, source_target_pairs={{0,2},{2,4},{4,6},{6,0},{1,3},{3,5},{5,7},{7,1},{8,10},{10,12},{12... | collective-permute-start | bytes 380936 | tf_op jit(solution)/shard_map/ppermute | solution.py:372
  106.4 8.9 %collective-permute-start.7 = (bf16[496,128]{1,0:T(8,128)(2,1)S(1)}, bf16[496,128]{1,0:T(8,128)(2,1)S(1)}, u32[]{:S(2)}, u32[]{:S(2)}) collective-permute-start(bf16[496,128]{1,0:T(8,128)(2,1)S(1)} %get-tuple-element.22), channel_id=1, source_target_pairs={{0,4},{2,6},{4,0},{6,2},{1,5},{3,7},{5,1},{7,3},{8,12},{10,14},{12... | collective-permute-start | bytes 380936 | tf_op jit(solution)/shard_map/ppermute | solution.py:372
  111.0 6.5 %collective-permute-start.8 = (bf16[496,128]{1,0:T(8,128)(2,1)S(1)}, bf16[496,128]{1,0:T(8,128)(2,1)S(1)}, u32[]{:S(2)}, u32[]{:S(2)}) collective-permute-start(bf16[496,128]{1,0:T(8,128)(2,1)S(1)} %get-tuple-element.23), channel_id=1, source_target_pairs={{0,6},{2,0},{4,2},{6,4},{1,7},{3,1},{5,3},{7,5},{8,14},{10,8},{12,... | collective-permute-start | bytes 380936 | tf_op jit(solution)/shard_map/ppermute | solution.py:372
  164.1 10.7 %copy-start.5 = (bf16[192,640]{1,0:T(8,128)(2,1)S(1)}, bf16[192,640]{1,0:T(8,128)(2,1)}, u32[]{:S(2)}) copy-start(bf16[192,640]{1,0:T(8,128)(2,1)} %copy-done.4) | copy-start | bytes 737284
  164.1 10.7 %copy-start.8 = (bf16[192,640]{1,0:T(8,128)(2,1)S(1)}, bf16[192,640]{1,0:T(8,128)(2,1)}, u32[]{:S(2)}) copy-start(bf16[192,640]{1,0:T(8,128)(2,1)} %copy-done.6) | copy-start | bytes 737284
  165.0 26.1 %all-to-all-start.3 = ((bf16[16,16,768]{2,1,0:T(8,128)(2,1)}), bf16[16,16,768]{2,1,0:T(8,128)(2,1)S(1)}, u32[]{:S(2)}, u32[]{:S(2)}) async-start(bf16[16,16,768]{2,1,0:T(8,128)(2,1)} %shard_map.124), calls=%async_computation.3 | async-start | bytes 786432 | tf_op jit(solution)/shard_map/all_to_all | solution.py:398
  (2 other events, 1.6 us)

commit v2 on v1

--- a/solution.py
+++ b/solution.py
@@ -27,7 +27,9 @@
     return pl.pallas_call(
         body,
         out_shape=outs,
-        in_specs=[SMEM if a.ndim == 1 else VMEM for a in args],
+        in_specs=[
+            SMEM if a.ndim == 1 else VMEM for a in args
+        ],
         out_specs=jax.tree.map(lambda _: VMEM, outs),
         scratch_shapes=scratch,
         compiler_params=pltpu.CompilerParams(vmem_limit_bytes=48 * 1024 * 1024),
@@ -52,67 +54,83 @@
 
 
 def scatter_kernel(per, live, act, grad, send):
-    tokens = act.shape[1]
+    tokens, width = act.shape[1:]
     x = lax.axis_index("x")
     off = jnp.int32(0)
     for b in range(live.shape[0] - 1):
         off = off + jnp.where(x > b, live[b], 0)
-    shape = (2 * tokens, tokens)
-    row = lax.broadcasted_iota(jnp.int32, shape, 0)
-    column = lax.broadcasted_iota(jnp.int32, shape, 1)
-    place = (row >> log2(2 * per) << log2(per)) + (row & (per - 1))
-    hot = ((place - (off & (tokens - 1)) + tokens) & (tokens - 1)) == column
-    is_up = (row & per) != 0
-    first = jnp.where(hot & ~is_up, 1.0, 0.0).astype(BF16)
-    second = jnp.where(hot & is_up, 1.0, 0.0).astype(BF16)
-    send[...] = (contract(first, act[0], 1, 0) + contract(second, grad[0], 1, 0)).astype(BF16)
+    row = lax.broadcasted_iota(jnp.int32, (tokens, tokens), 0)
+    column = lax.broadcasted_iota(jnp.int32, (tokens, tokens), 1)
+    roll = ((row - column - off) & (tokens - 1)) == 0
+    roll = jnp.where(roll, 1.0, 0.0).astype(BF16)
+    groups = (tokens // per, per, width)
+    first = contract(roll, act[0], 1, 0).reshape(groups)
+    second = contract(roll, grad[0], 1, 0).reshape(groups)
+    send[...] = jnp.concatenate([first, second], axis=1).reshape(2 * tokens, width).astype(BF16)
 
 
 TAIL = 16
 
 
-def terms_kernel(nums, own, right, left, over_in, over_up, gain, ahead, behind, rest, keep, send):
-    core = nums[CORE]
+def terms_of(inputs, upstream, gain, ahead, behind, rest, tail_ref):
     gain_wide = gain[...].astype(F32)
-    n = over_in.shape[0]
+    n = inputs.shape[0]
     chunk = n // 2
-    ones = jnp.ones(rest.shape, BF16)
-    for k in range(4):
-        inputs, upstream = pick((own, right, left, over_in, over_up), k)
-        wide = inputs.astype(F32)
-        scaled = (wide * gain_wide).astype(BF16)
-        main = contract(scaled, ahead[...], 1, 1) + contract(upstream, behind[...], 1, 1)
-        main = main.astype(BF16)
-        squares = wide * wide
-        high = squares.astype(BF16)
-        low = (squares - high.astype(F32)).astype(BF16)
-        tails = []
+    extra = rest.shape[0]
+    wide = inputs.astype(F32)
+    scaled = (wide * gain_wide).astype(BF16)
+    main = contract(scaled, ahead[...], 1, 1) + contract(upstream, behind[...], 1, 1)
+    main = main.astype(BF16)
+    squares = jnp.sum(wide * wide, axis=1, keepdims=True)
+    high = squares.astype(BF16).astype(F32)
+    tail_ref[...] = jnp.zeros(tail_ref.shape, F32)
+    tail_ref[:, :extra] = contract(upstream, rest[...], 1, 1)
+    tail_ref[:, extra : extra + 1] = high
+    tail_ref[:, extra + 1 : extra + 2] = squares - high
+    tails = [tail_ref[h * chunk : (h + 1) * chunk, :].T[:TAIL].astype(BF16) for h in range(2)]
+
+    def store(out):
         for h in range(2):
-            r = slice(h * chunk, (h + 1) * chunk)
-            total = contract(ones, high[r], 1, 1) + contract(ones, low[r], 1, 1)
-            total_hi = total.astype(BF16).astype(F32)
-            row = lax.broadcasted_iota(jnp.int32, total.shape, 0)
-            total = jnp.where(row == 0, total_hi, jnp.where(row == 1, total - total_hi, 0.0))
-            tails.append(jnp.concatenate([contract(rest[...], upstream[r], 1, 1), total], axis=0).astype(BF16))
-
-        def store(out):
-            for h in range(2):
-                at = (k % 2) * 2 + h
-                for i in range(main.shape[1] // 128):
-                    out[at, i * chunk : (i + 1) * chunk, :] = main[
-                        h * chunk : (h + 1) * chunk, i * 128 : (i + 1) * 128
-                    ]
-                out[at, -TAIL:, :] = jnp.zeros((TAIL, 128), BF16)
-                out[at, -TAIL:, :chunk] = tails[h]
-
-        pl.when(core == k // 2)(functools.partial(store, keep))
-        pl.when(core != k // 2)(functools.partial(store, send))
-
-
-def pair_kernel(nums, keep, recv, *outs):
+            for i in range(main.shape[1] // 128):
+                out[h, i * chunk : (i + 1) * chunk, :] = main[
+                    h * chunk : (h + 1) * chunk, i * 128 : (i + 1) * 128
+                ]
+            out[h, -TAIL:, :] = jnp.zeros((TAIL, 128), BF16)
+            out[h, -TAIL:, :chunk] = tails[h]
+
+    return store
+
+
+def by_core(nums, store, first, second):
+    pl.when(nums[CORE] == 0)(functools.partial(store, first))
+    pl.when(nums[CORE] != 0)(functools.partial(store, second))
+
+
+def early_kernel(nums, own, right, left, gain, ahead, behind, rest, keep, send, middle, *tail_refs):
+    weights = (gain, ahead, behind, rest)
+    by_core(nums, terms_of(own[0], own[1], *weights, tail_refs[0]), keep, send)
+    by_core(nums, terms_of(left[0], left[1], *weights, tail_refs[1]), send, keep)
+    terms_of(right[0], right[1], *weights, tail_refs[2])(middle)
+
+
+def late_kernel(nums, middle, over_in, over_up, gain, ahead, behind, rest, keep, send, tail_ref):
+    def passed(out):
+        out[...] = middle[...]
+
+    by_core(nums, passed, keep, send)
+    store = terms_of(over_in[...], over_up[...], gain, ahead, behind, rest, tail_ref)
+    by_core(nums, store, send, keep)
+
+
+def pair_kernel(nums, keep_a, keep_b, recv_a, recv_b, *outs):
     for i, out in enumerate(outs):
         chunk = (nums[LINE] + i) & (len(outs) - 1)
-        out[...] = (keep[chunk].astype(F32) + recv[chunk].astype(F32)).astype(BF16)
+
+        def add(keep, recv, out=out, at=chunk & 1):
+            out[...] = (keep[at].astype(F32) + recv[at].astype(F32)).astype(BF16)
+
+        pl.when(chunk < 2)(functools.partial(add, keep_a, recv_a))
+        pl.when(chunk >= 2)(functools.partial(add, keep_b, recv_b))
 
 
 def point_kernel(hid, features, *refs):
@@ -360,14 +378,20 @@
     own_count = live // nc // nzl
     size = own_count * (width // 128) + TAIL
     product = 2 * live * width * WIDE
-    halves = shape(nzl, size, 128)
-    keep, give = call(
-        terms_kernel, (halves, halves), [], 5 * product,
-        nums, *blocks, gain, ahead_rows, behind_rows, rest_rows,
-    )
-    taken = lax.ppermute(give, "c", [(0, 1), (1, 0)])
+    two = shape(2, size, 128)
+    weights = (gain, ahead_rows, behind_rows, rest_rows)
+    tail_ref = pltpu.VMEM((part, 128), F32)
+    swap = [(0, 1), (1, 0)]
+    keep_a, give_a, middle = call(
+        early_kernel, (two,) * 3, [tail_ref] * 3, 4 * product, nums, own, right, left, *weights
+    )
+    taken_a = lax.ppermute(give_a, "c", swap)
+    keep_b, give_b = call(
+        late_kernel, (two,) * 2, [tail_ref], product, nums, middle, over_in, over_up, *weights
+    )
+    taken_b = lax.ppermute(give_b, "c", swap)
     chunk = shape(size, 128)
-    pairs = call(pair_kernel, (chunk,) * nzl, [], nzl * size * 128, nums, keep, taken)
+    pairs = call(pair_kernel, (chunk,) * nzl, [], nzl * size * 128, nums, keep_a, keep_b, taken_a, taken_b)
     others = [
         lax.ppermute(pairs[i], "zl", [(a, (a + i) % nzl) for a in range(nzl)]) for i in range(1, nzl)
     ]

time: 194 us -> 189 us (0.974)
  local copies, waits for them, and re-layouts: 6.83 us -> 3.77 us
  blocking collectives: 42 us -> 39.8 us
    ppermute x1, waiting for transfers between devices: 1.99 us -> 0.01 us  [per_device(): over_up = lax.ppermute(left[1], 'x', back)]
    ppermute x1 -> x2, starting transfers between devices: 8.57 us -> 9.87 us  [the longest x1 7.95 us: per_device(): taken_a = lax.ppermute(give_a, 'c', swap)]
    pallas_call x8 -> x9, Pallas kernels: 15.8 us -> 15.9 us  [call(): pl.pallas_call(body, out_shape=outs, in_specs=[SMEM if a.ndim == 1 else V...]
  transfers between devices with their start and end apart: 12 -> 13, of which waited for: 8 -> 8; matrix products, arithmetic and copies ran while one was open for 2% -> 0% of each run, Pallas kernels for 1% -> 4%
where the time goes in v2:
time: 189 us; the launch traced here: 187 us
  starting transfers between devices  69.8 us (37%)
  waiting for transfers between devices  54.5 us (29%)
  blocking collectives  39.8 us (21%)
  Pallas kernels  15.9 us (8%)
  local copies, waits for them, and re-layouts  3.77 us (2%)
    all_to_all x1, blocking collectives, per_device(): out = lax.all_to_all(out, 'x', 0, 0, tiled=True)  20.7 us
    all_gather x1, blocking collectives, per_device(): every = lax.all_gather(point, ('zl', 'c'), axis=0, tiled=True)  19.1 us
    all_to_all x1, waiting for transfers between devices, per_device(): lax.all_to_all(send, ('y', 'x'), 0, 0, tiled=True)  18.2 us
    pallas_call x9, Pallas kernels, call(): pl.pallas_call(body, out_shape=outs, in_specs=[SMEM if a.ndim == 1 else V...  15.9 us
    all_to_all x1, waiting for transfers between devices, per_device(): out = lax.all_to_all(out, ('y', 'zh'), 0, 0, tiled=True)  13.7 us
    all_to_all x1, waiting for transfers between devices, per_device(): column = lax.all_to_all(copies, 'y', 0, 0, tiled=True)  12.6 us
    ppermute x3, starting transfers between devices, per_device(): lax.ppermute(pairs[i], 'zl', [(a, (a + i) % nzl) for a in range(nzl)])  12 us
    ppermute x1, starting transfers between devices, per_device(): other = lax.ppermute(packed, 'zh', [(0, 1), (1, 0)])  10.6 us
  transfers between devices with their start and end apart: 13, of which 8 were waited for; matrix products, arithmetic and copies ran while one was open for 0% of the time, Pallas kernels for 4%

profile of v2, /device:TPU:1, one launch (start us, length us, event | category | flops | bytes accessed | tf_op | source)
XLA Modules:
  0.0 187.3 jit_solution(14199423774661595301)
XLA Ops:
  3.2 1.8 shard_map.119
  5.0 10.5 %all-to-all-start = ((bf16[32,16,640]{2,1,0:T(8,128)(2,1)}), bf16[32,16,640]{2,1,0:T(8,128)(2,1)S(1)}, u32[]{:S(2)}, u32[]{:S(2)}) async-start(bf16[32,16,640]{2,1,0:T(8,128)(2,1)} %bitcast.5), calls=%async_computation | async-start | bytes 1310720 | tf_op jit(solution)/shard_map/all_to_all | solution.py:334
  16.0 18.2 %all-to-all-done = bf16[32,16,640]{2,1,0:T(8,128)(2,1)S(1)} async-done(((bf16[32,16,640]{2,1,0:T(8,128)(2,1)}), bf16[32,16,640]{2,1,0:T(8,128)(2,1)S(1)}, u32[]{:S(2)}, u32[]{:S(2)}) %all-to-all-start) | async-done | bytes 655392 | tf_op jit(solution)/shard_map/all_to_all | solution.py:334
  34.3 10.6 %collective-permute-start = (bf16[48,640]{1,0:T(8,128)(2,1)S(1)}, bf16[48,640]{1,0:T(8,128)(2,1)S(1)}, u32[]{:S(2)}, u32[]{:S(2)}) collective-permute-start(bf16[48,640]{1,0:T(8,128)(2,1)S(1)} %bitcast.35), channel_id=1, source_target_pairs={{0,32},{32,0},{1,33},{33,1},{2,34},{34,2},{3,35},{35,3},{4,36},{36... | collective-permute-start | bytes 184328 | tf_op jit(solution)/shard_map/ppermute | solution.py:353
  45.0 1.6 collective-permute-done
  47.5 3.5 %all-to-all-start.1 = ((bf16[8,48,640]{2,1,0:T(8,128)(2,1)}), bf16[8,48,640]{2,1,0:T(8,128)(2,1)S(1)}, u32[]{:S(2)}, u32[]{:S(2)}) async-start(bf16[8,48,640]{2,1,0:T(8,128)(2,1)} %broadcast_in_dim.59), calls=%async_computation.1 | async-start | bytes 983040 | tf_op jit(solution)/shard_map/all_to_all | solution.py:357
  51.0 12.6 %all-to-all-done.1 = bf16[8,48,640]{2,1,0:T(8,128)(2,1)S(1)} async-done(((bf16[8,48,640]{2,1,0:T(8,128)(2,1)}), bf16[8,48,640]{2,1,0:T(8,128)(2,1)S(1)}, u32[]{:S(2)}, u32[]{:S(2)}) %all-to-all-start.1) | async-done | bytes 491552 | tf_op jit(solution)/shard_map/all_to_all | solution.py:357
  64.7 3.5 %collective-permute-start.1 = (bf16[2,192,640]{2,1,0:T(8,128)(2,1)S(1)}, bf16[2,192,640]{2,1,0:T(8,128)(2,1)S(1)}, u32[]{:S(2)}, u32[]{:S(2)}) collective-permute-start(bf16[2,192,640]{2,1,0:T(8,128)(2,1)S(1)} %bitcast.25), channel_id=1, source_target_pairs={{0,8},{8,16},{16,24},{24,0},{1,9},{9,17},{17,25},{25,1},{2,10},{10... | collective-permute-start | bytes 1474568 | tf_op jit(solution)/shard_map/ppermute | solution.py:366
  68.3 3.5 %collective-permute-start.2 = (bf16[2,192,640]{2,1,0:T(8,128)(2,1)S(1)}, bf16[2,192,640]{2,1,0:T(8,128)(2,1)S(1)}, u32[]{:S(2)}, u32[]{:S(2)}) collective-permute-start(bf16[2,192,640]{2,1,0:T(8,128)(2,1)S(1)} %bitcast.26), channel_id=1, source_target_pairs={{0,24},{8,0},{16,8},{24,16},{1,25},{9,1},{17,9},{25,17},{2,26},{10... | collective-permute-start | bytes 1474568 | tf_op jit(solution)/shard_map/ppermute | solution.py:367
  72.1 4.4 %collective-permute-done.1.right = bf16[2,192,640]{2,1,0:T(8,128)(2,1)S(1)} collective-permute-done((bf16[2,192,640]{2,1,0:T(8,128)(2,1)S(1)}, bf16[2,192,640]{2,1,0:T(8,128)(2,1)S(1)}, u32[]{:S(2)}, u32[]{:S(2)}) %collective-permute-start.1) | collective-permute-done | bytes 491552 | tf_op jit(solution)/shard_map/ppermute | solution.py:366
  76.5 2.0 %collective-permute-start.3 = (bf16[192,640]{1,0:T(8,128)(2,1)S(1)}, bf16[192,640]{1,0:T(8,128)(2,1)S(1)}, u32[]{:S(2)}, u32[]{:S(2)}) collective-permute-start(bf16[192,640]{1,0:T(8,128)(2,1)S(1)} %slice_bitcast_fusion.1), channel_id=1, source_target_pairs={{0,8},{8,16},{16,24},{24,0},{1,9},{9,17},{17,25},{25,1},{2,10},{10... | collective-permute-start | bytes 737288 | tf_op jit(solution)/shard_map/ppermute | solution.py:368
  78.6 4.5 %collective-permute-start.4 = (bf16[192,640]{1,0:T(8,128)(2,1)S(1)}, bf16[192,640]{1,0:T(8,128)(2,1)S(1)}, u32[]{:S(2)}, u32[]{:S(2)}) collective-permute-start(bf16[192,640]{1,0:T(8,128)(2,1)S(1)} %slice_bitcast_fusion), channel_id=1, source_target_pairs={{0,24},{8,0},{16,8},{24,16},{1,25},{9,1},{17,9},{25,17},{2,26},{10... | collective-permute-start | bytes 737288 | tf_op jit(solution)/shard_map/ppermute | solution.py:369
  83.3 3.2 %shard_map.120 = (bf16[2,496,128]{2,1,0:T(8,128)(2,1)S(1)}, bf16[2,496,128]{2,1,0:T(8,128)(2,1)S(1)}, bf16[2,496,128]{2,1,0:T(8,128)(2,1)S(1)}) custom-call(s32[12]{0:T(128)S(1)} %concatenate.13.nums, bf16[2,192,640]{2,1,0:T(8,128)(2,1)S(1)} %bitcast.27, bf16[2,192,640]{2,1,0:T(8,128)(2,1)S(1)} %collective-permute-done.1.right, ...), custom_call_target="tpu_custom_call" | custom-call | flops 1006632960 | bytes 3886384 | tf_op jit(solution)/shard_map/pallas_call | solution.py:27
  86.5 7.9 %collective-permute-start.5 = (bf16[2,496,128]{2,1,0:T(8,128)(2,1)S(1)}, bf16[2,496,128]{2,1,0:T(8,128)(2,1)S(1)}, u32[]{:S(2)}, u32[]{:S(2)}) collective-permute-start(bf16[2,496,128]{2,1,0:T(8,128)(2,1)S(1)} %get-tuple-element.24), channel_id=1, source_target_pairs={{0,1},{1,0},{2,3},{3,2},{4,5},{5,4},{6,7},{7,6},{8,9},{9,8},{10,11... | collective-permute-start | bytes 761864 | tf_op jit(solution)/shard_map/ppermute | solution.py:388
  95.9 1.9 %collective-permute-start.6 = (bf16[2,496,128]{2,1,0:T(8,128)(2,1)S(1)}, bf16[2,496,128]{2,1,0:T(8,128)(2,1)S(1)}, u32[]{:S(2)}, u32[]{:S(2)}) collective-permute-start(bf16[2,496,128]{2,1,0:T(8,128)(2,1)S(1)} %get-tuple-element.25), channel_id=1, source_target_pairs={{0,1},{1,0},{2,3},{3,2},{4,5},{5,4},{6,7},{7,6},{8,9},{9,8},{10,11... | collective-permute-start | bytes 761864 | tf_op jit(solution)/shard_map/ppermute | solution.py:392
  100.0 3.0 %collective-permute-start.7 = (bf16[496,128]{1,0:T(8,128)(2,1)S(1)}, bf16[496,128]{1,0:T(8,128)(2,1)S(1)}, u32[]{:S(2)}, u32[]{:S(2)}) collective-permute-start(bf16[496,128]{1,0:T(8,128)(2,1)S(1)} %get-tuple-element.27), channel_id=1, source_target_pairs={{0,2},{2,4},{4,6},{6,0},{1,3},{3,5},{5,7},{7,1},{8,10},{10,12},{12... | collective-permute-start | bytes 380936 | tf_op jit(solution)/shard_map/ppermute | solution.py:396
  103.1 4.7 %collective-permute-start.8 = (bf16[496,128]{1,0:T(8,128)(2,1)S(1)}, bf16[496,128]{1,0:T(8,128)(2,1)S(1)}, u32[]{:S(2)}, u32[]{:S(2)}) collective-permute-start(bf16[496,128]{1,0:T(8,128)(2,1)S(1)} %get-tuple-element.28), channel_id=1, source_target_pairs={{0,4},{2,6},{4,0},{6,2},{1,5},{3,7},{5,1},{7,3},{8,12},{10,14},{12... | collective-permute-start | bytes 380936 | tf_op jit(solution)/shard_map/ppermute | solution.py:396
  107.8 4.3 %collective-permute-start.9 = (bf16[496,128]{1,0:T(8,128)(2,1)S(1)}, bf16[496,128]{1,0:T(8,128)(2,1)S(1)}, u32[]{:S(2)}, u32[]{:S(2)}) collective-permute-start(bf16[496,128]{1,0:T(8,128)(2,1)S(1)} %get-tuple-element.29), channel_id=1, source_target_pairs={{0,6},{2,0},{4,2},{6,4},{1,7},{3,1},{5,3},{7,5},{8,14},{10,8},{12,... | collective-permute-start | bytes 380936 | tf_op jit(solution)/shard_map/ppermute | solution.py:396
  115.1 19.1 %all_gather.3.every = bf16[3968,128]{1,0:T(8,128)(2,1)S(1)} all-gather(bf16[496,128]{1,0:T(8,128)(2,1)S(1)} %shard_map.123), channel_id=1, replica_groups=mesh['y'=8,'zh'=2,'x'=4,'zl'=4,'c'=2] {'zl','c'}, dimensions={0}, use_global_device_ids=true | all-gather | bytes 1142784 | tf_op jit(solution)/shard_map/all_gather | solution.py:407
  134.2 4.0 %shard_map.124 = (bf16[4,272,640]{2,1,0:T(8,128)(2,1)S(1)}, bf16[16,640]{1,0:T(8,128)(2,1)S(1)}) custom-call(s32[12]{0:T(128)S(1)} %concatenate.13.nums, bf16[2,192,640]{2,1,0:T(8,128)(2,1)S(1)} %bitcast.28, bf16[2,192,640]{2,1,0:T(8,128)(2,1)S(1)} %collective-permute-done.1.right, bf16[2,192,640]{2,1,0:T(8,128)(2,1)S(1)} %collective-permute-done.2.left, ...), custom_call_target="tpu_custom_call" | custom-call | flops 1258291200 | bytes 4949296 | tf_op jit(solution)/shard_map/pallas_call | solution.py:27
  138.3 20.7 %all_to_all.28.parts = bf16[4,272,640]{2,1,0:T(8,128)(2,1)S(1)} all-to-all(bf16[4,272,640]{2,1,0:T(8,128)(2,1)S(1)} %get-tuple-element.30), channel_id=1, replica_groups=mesh['y'=8,'zh'=2,'x'=4,'zl'=4,'c'=2] {'x'}, dimensions={0} | all-to-all | bytes 2785280 | tf_op jit(solution)/shard_map/all_to_all | solution.py:418
  159.9 9.8 %all-to-all-start.3 = ((bf16[16,16,768]{2,1,0:T(8,128)(2,1)}), bf16[16,16,768]{2,1,0:T(8,128)(2,1)S(1)}, u32[]{:S(2)}, u32[]{:S(2)}) async-start(bf16[16,16,768]{2,1,0:T(8,128)(2,1)} %shard_map.125), calls=%async_computation.3 | async-start | bytes 786432 | tf_op jit(solution)/shard_map/all_to_all | solution.py:422
  169.7 2.6 %shard_map.127 = (bf16[216,640]{1,0:T(8,128)(2,1)}, bf16[216,640]{1,0:T(8,128)(2,1)}, bf16[216,640]{1,0:T(8,128)(2,1)}) custom-call(bf16[2,192,640]{2,1,0:T(8,128)(2,1)S(1)} %bitcast.29, bf16[2,192,640]{2,1,0:T(8,128)(2,1)S(1)} %collective-permute-done.1.right, bf16[2,192,640]{2,1,0:T(8,128)(2,1)S(1)} %collective-permute-done.2.left, ...), custom_call_target="tpu_custom_call" | custom-call | flops 754974720 | bytes 3812608 | tf_op jit(solution)/shard_map/pallas_call | solution.py:27
  172.4 13.7 %all-to-all-done.3.parts = bf16[16,16,768]{2,1,0:T(8,128)(2,1)S(1)} async-done(((bf16[16,16,768]{2,1,0:T(8,128)(2,1)}), bf16[16,16,768]{2,1,0:T(8,128)(2,1)S(1)}, u32[]{:S(2)}, u32[]{:S(2)}) %all-to-all-start.3) | async-done | bytes 393248 | tf_op jit(solution)/shard_map/all_to_all | solution.py:422
  (60 shorter events, 14.3 us)
Async XLA Ops:
  0.6 1.0 copy-start
  1.6 1.0 copy-start.1
  2.6 0.7 copy-start.6
  3.2 12.3 %copy-start.10 = (s32[16]{0:T(128)S(1)}, s32[16]{0:T(128)}, u32[]{:S(2)}) copy-start(s32[16]{0:T(128)} %param.10) | copy-start | bytes 196
  3.2 12.5 %copy-start.7 = (s32[4]{0:T(128)S(1)}, s32[4]{0:T(128)}, u32[]{:S(2)}) copy-start(s32[4]{0:T(128)} %live.1) | copy-start | bytes 52
  5.0 29.2 %all-to-all-start = ((bf16[32,16,640]{2,1,0:T(8,128)(2,1)}), bf16[32,16,640]{2,1,0:T(8,128)(2,1)S(1)}, u32[]{:S(2)}, u32[]{:S(2)}) async-start(bf16[32,16,640]{2,1,0:T(8,128)(2,1)} %bitcast.5), calls=%async_computation | async-start | bytes 1310720 | tf_op jit(solution)/shard_map/all_to_all | solution.py:334
  34.3 12.3 %collective-permute-start = (bf16[48,640]{1,0:T(8,128)(2,1)S(1)}, bf16[48,640]{1,0:T(8,128)(2,1)S(1)}, u32[]{:S(2)}, u32[]{:S(2)}) collective-permute-start(bf16[48,640]{1,0:T(8,128)(2,1)S(1)} %bitcast.35), channel_id=1, source_target_pairs={{0,32},{32,0},{1,33},{33,1},{2,34},{34,2},{3,35},{35,3},{4,36},{36... | collective-permute-start | bytes 184328 | tf_op jit(solution)/shard_map/ppermute | solution.py:353
  47.5 16.2 %all-to-all-start.1 = ((bf16[8,48,640]{2,1,0:T(8,128)(2,1)}), bf16[8,48,640]{2,1,0:T(8,128)(2,1)S(1)}, u32[]{:S(2)}, u32[]{:S(2)}) async-start(bf16[8,48,640]{2,1,0:T(8,128)(2,1)} %broadcast_in_dim.59), calls=%async_computation.1 | async-start | bytes 983040 | tf_op jit(solution)/shard_map/all_to_all | solution.py:357
  63.7 8.1 %copy-start.8 = (bf16[216,640]{1,0:T(8,128)(2,1)S(1)}, bf16[216,640]{1,0:T(8,128)(2,1)}, u32[]{:S(2)}) copy-start(bf16[216,640]{1,0:T(8,128)(2,1)} %param.14) | copy-start | bytes 829444
  63.7 8.2 %copy-start.9 = (bf16[640]{0:T(1024)(128)(2,1)S(1)}, bf16[640]{0:T(1024)(128)(2,1)}, u32[]{:S(2)}) copy-start(bf16[640]{0:T(1024)(128)(2,1)} %param.15) | copy-start | bytes 3844
  64.7 18.3 %copy-start.2 = (bf16[640,216]{0,1:T(8,128)(2,1)S(1)}, bf16[640,216]{0,1:T(8,128)(2,1)}, u32[]{:S(2)}) copy-start(bf16[640,216]{0,1:T(8,128)(2,1)} %param.13) | copy-start | bytes 829444
  64.7 18.3 %copy-start.4 = (bf16[640,216]{0,1:T(8,128)(2,1)S(1)}, bf16[640,216]{0,1:T(8,128)(2,1)}, u32[]{:S(2)}) copy-start(bf16[640,216]{0,1:T(8,128)(2,1)} %param.12) | copy-start | bytes 829444
  64.7 11.7 %collective-permute-start.1 = (bf16[2,192,640]{2,1,0:T(8,128)(2,1)S(1)}, bf16[2,192,640]{2,1,0:T(8,128)(2,1)S(1)}, u32[]{:S(2)}, u32[]{:S(2)}) collective-permute-start(bf16[2,192,640]{2,1,0:T(8,128)(2,1)S(1)} %bitcast.25), channel_id=1, source_target_pairs={{0,8},{8,16},{16,24},{24,0},{1,9},{9,17},{17,25},{25,1},{2,10},{10... | collective-permute-start | bytes 1474568 | tf_op jit(solution)/shard_map/ppermute | solution.py:366
  68.3 10.3 %collective-permute-start.2 = (bf16[2,192,640]{2,1,0:T(8,128)(2,1)S(1)}, bf16[2,192,640]{2,1,0:T(8,128)(2,1)S(1)}, u32[]{:S(2)}, u32[]{:S(2)}) collective-permute-start(bf16[2,192,640]{2,1,0:T(8,128)(2,1)S(1)} %bitcast.26), channel_id=1, source_target_pairs={{0,24},{8,0},{16,8},{24,16},{1,25},{9,1},{17,9},{25,17},{2,26},{10... | collective-permute-start | bytes 1474568 | tf_op jit(solution)/shard_map/ppermute | solution.py:367
  76.5 17.9 %collective-permute-start.3 = (bf16[192,640]{1,0:T(8,128)(2,1)S(1)}, bf16[192,640]{1,0:T(8,128)(2,1)S(1)}, u32[]{:S(2)}, u32[]{:S(2)}) collective-permute-start(bf16[192,640]{1,0:T(8,128)(2,1)S(1)} %slice_bitcast_fusion.1), channel_id=1, source_target_pairs={{0,8},{8,16},{16,24},{24,0},{1,9},{9,17},{17,25},{25,1},{2,10},{10... | collective-permute-start | bytes 737288 | tf_op jit(solution)/shard_map/ppermute | solution.py:368
  78.6 15.8 %collective-permute-start.4 = (bf16[192,640]{1,0:T(8,128)(2,1)S(1)}, bf16[192,640]{1,0:T(8,128)(2,1)S(1)}, u32[]{:S(2)}, u32[]{:S(2)}) collective-permute-start(bf16[192,640]{1,0:T(8,128)(2,1)S(1)} %slice_bitcast_fusion), channel_id=1, source_target_pairs={{0,24},{8,0},{16,8},{24,16},{1,25},{9,1},{17,9},{25,17},{2,26},{10... | collective-permute-start | bytes 737288 | tf_op jit(solution)/shard_map/ppermute | solution.py:369
  86.5 11.4 %collective-permute-start.5 = (bf16[2,496,128]{2,1,0:T(8,128)(2,1)S(1)}, bf16[2,496,128]{2,1,0:T(8,128)(2,1)S(1)}, u32[]{:S(2)}, u32[]{:S(2)}) collective-permute-start(bf16[2,496,128]{2,1,0:T(8,128)(2,1)S(1)} %get-tuple-element.24), channel_id=1, source_target_pairs={{0,1},{1,0},{2,3},{3,2},{4,5},{5,4},{6,7},{7,6},{8,9},{9,8},{10,11... | collective-permute-start | bytes 761864 | tf_op jit(solution)/shard_map/ppermute | solution.py:388
  95.9 3.4 %collective-permute-start.6 = (bf16[2,496,128]{2,1,0:T(8,128)(2,1)S(1)}, bf16[2,496,128]{2,1,0:T(8,128)(2,1)S(1)}, u32[]{:S(2)}, u32[]{:S(2)}) collective-permute-start(bf16[2,496,128]{2,1,0:T(8,128)(2,1)S(1)} %get-tuple-element.25), channel_id=1, source_target_pairs={{0,1},{1,0},{2,3},{3,2},{4,5},{5,4},{6,7},{7,6},{8,9},{9,8},{10,11... | collective-permute-start | bytes 761864 | tf_op jit(solution)/shard_map/ppermute | solution.py:392
  99.3 34.9 %copy-start.3 = (bf16[640,216]{0,1:T(8,128)(2,1)S(1)}, bf16[640,216]{0,1:T(8,128)(2,1)}, u32[]{:S(2)}) copy-start(bf16[640,216]{0,1:T(8,128)(2,1)} %param.13) | copy-start | bytes 829444
  99.3 34.9 %copy-start.5 = (bf16[640,216]{0,1:T(8,128)(2,1)S(1)}, bf16[640,216]{0,1:T(8,128)(2,1)}, u32[]{:S(2)}) copy-start(bf16[640,216]{0,1:T(8,128)(2,1)} %param.12) | copy-start | bytes 829444
  100.0 12.0 %collective-permute-start.7 = (bf16[496,128]{1,0:T(8,128)(2,1)S(1)}, bf16[496,128]{1,0:T(8,128)(2,1)S(1)}, u32[]{:S(2)}, u32[]{:S(2)}) collective-permute-start(bf16[496,128]{1,0:T(8,128)(2,1)S(1)} %get-tuple-element.27), channel_id=1, source_target_pairs={{0,2},{2,4},{4,6},{6,0},{1,3},{3,5},{5,7},{7,1},{8,10},{10,12},{12... | collective-permute-start | bytes 380936 | tf_op jit(solution)/shard_map/ppermute | solution.py:396
  103.1 10.5 %collective-permute-start.8 = (bf16[496,128]{1,0:T(8,128)(2,1)S(1)}, bf16[496,128]{1,0:T(8,128)(2,1)S(1)}, u32[]{:S(2)}, u32[]{:S(2)}) collective-permute-start(bf16[496,128]{1,0:T(8,128)(2,1)S(1)} %get-tuple-element.28), channel_id=1, source_target_pairs={{0,4},{2,6},{4,0},{6,2},{1,5},{3,7},{5,1},{7,3},{8,12},{10,14},{12... | collective-permute-start | bytes 380936 | tf_op jit(solution)/shard_map/ppermute | solution.py:396
  107.8 6.8 %collective-permute-start.9 = (bf16[496,128]{1,0:T(8,128)(2,1)S(1)}, bf16[496,128]{1,0:T(8,128)(2,1)S(1)}, u32[]{:S(2)}, u32[]{:S(2)}) collective-permute-start(bf16[496,128]{1,0:T(8,128)(2,1)S(1)} %get-tuple-element.29), channel_id=1, source_target_pairs={{0,6},{2,0},{4,2},{6,4},{1,7},{3,1},{5,3},{7,5},{8,14},{10,8},{12,... | collective-permute-start | bytes 380936 | tf_op jit(solution)/shard_map/ppermute | solution.py:396
  159.9 26.1 %all-to-all-start.3 = ((bf16[16,16,768]{2,1,0:T(8,128)(2,1)}), bf16[16,16,768]{2,1,0:T(8,128)(2,1)S(1)}, u32[]{:S(2)}, u32[]{:S(2)}) async-start(bf16[16,16,768]{2,1,0:T(8,128)(2,1)} %shard_map.125), calls=%async_computation.3 | async-start | bytes 786432 | tf_op jit(solution)/shard_map/all_to_all | solution.py:422

commit v3 on v2

--- a/solution.py
+++ b/solution.py
@@ -124,7 +124,7 @@
 
 def pair_kernel(nums, keep_a, keep_b, recv_a, recv_b, *outs):
     for i, out in enumerate(outs):
-        chunk = (nums[LINE] + i) & (len(outs) - 1)
+        chunk = nums[LINE] ^ i
 
         def add(keep, recv, out=out, at=chunk & 1):
             out[...] = (keep[at].astype(F32) + recv[at].astype(F32)).astype(BF16)
@@ -393,7 +393,7 @@
     chunk = shape(size, 128)
     pairs = call(pair_kernel, (chunk,) * nzl, [], nzl * size * 128, nums, keep_a, keep_b, taken_a, taken_b)
     others = [
-        lax.ppermute(pairs[i], "zl", [(a, (a + i) % nzl) for a in range(nzl)]) for i in range(1, nzl)
+        lax.ppermute(pairs[i], "zl", [(a, a ^ i) for a in range(nzl)]) for i in range(1, nzl)
     ]
     point = call(
         functools.partial(point_kernel, hid, features), chunk,

time: 189 us -> 190 us (level)
  starting transfers between devices: 69.8 us -> 66.4 us
  waiting for transfers between devices: 54.5 us -> 57.1 us
  blocking collectives: 39.8 us -> 41.7 us
    ppermute x3, waiting for transfers between devices: 2.52 us -> 5.14 us  [per_device(): lax.ppermute(pairs[i], 'zl', [(a, a ^ i) for a in range(nzl)])]
    all_to_all x1, starting transfers between devices: 9.83 us -> 7.61 us  [per_device(): out = lax.all_to_all(out, ('y', 'zh'), 0, 0, tiled=True)]
    all_gather x1, blocking collectives: 19.1 us -> 21.1 us  [per_device(): every = lax.all_gather(point, ('zl', 'c'), axis=0, tiled=True)]
where the time goes in v3:
time: 190 us; the launch traced here: 188 us
  starting transfers between devices  66.4 us (35%)
  waiting for transfers between devices  57.1 us (30%)
  blocking collectives  41.7 us (22%)
  Pallas kernels  15.9 us (8%)
  local copies, waits for them, and re-layouts  3.77 us (2%)
    all_gather x1, blocking collectives, per_device(): every = lax.all_gather(point, ('zl', 'c'), axis=0, tiled=True)  21.1 us
    all_to_all x1, blocking collectives, per_device(): out = lax.all_to_all(out, 'x', 0, 0, tiled=True)  20.6 us
    all_to_all x1, waiting for transfers between devices, per_device(): lax.all_to_all(send, ('y', 'x'), 0, 0, tiled=True)  18.2 us
    pallas_call x9, Pallas kernels, call(): pl.pallas_call(body, out_shape=outs, in_specs=[SMEM if a.ndim == 1 else V...  15.9 us
    all_to_all x1, waiting for transfers between devices, per_device(): out = lax.all_to_all(out, ('y', 'zh'), 0, 0, tiled=True)  13.7 us
    all_to_all x1, waiting for transfers between devices, per_device(): column = lax.all_to_all(copies, 'y', 0, 0, tiled=True)  12.6 us
    ppermute x3, starting transfers between devices, per_device(): lax.ppermute(pairs[i], 'zl', [(a, a ^ i) for a in range(nzl)])  10.8 us
    ppermute x1, starting transfers between devices, per_device(): other = lax.ppermute(packed, 'zh', [(0, 1), (1, 0)])  10.6 us
  transfers between devices with their start and end apart: 13, of which 8 were waited for; matrix products, arithmetic and copies ran while one was open for 0% of the time, Pallas kernels for 4%

profile of v3, /device:TPU:1, one launch (start us, length us, event | category | flops | bytes accessed | tf_op | source)
XLA Modules:
  0.0 188.4 jit_solution(254543302949699237)
XLA Ops:
  5.0 10.5 %all-to-all-start = ((bf16[32,16,640]{2,1,0:T(8,128)(2,1)}), bf16[32,16,640]{2,1,0:T(8,128)(2,1)S(1)}, u32[]{:S(2)}, u32[]{:S(2)}) async-start(bf16[32,16,640]{2,1,0:T(8,128)(2,1)} %bitcast.5), calls=%async_computation | async-start | bytes 1310720 | tf_op jit(solution)/shard_map/all_to_all | solution.py:334
  16.0 18.2 %all-to-all-done = bf16[32,16,640]{2,1,0:T(8,128)(2,1)S(1)} async-done(((bf16[32,16,640]{2,1,0:T(8,128)(2,1)}), bf16[32,16,640]{2,1,0:T(8,128)(2,1)S(1)}, u32[]{:S(2)}, u32[]{:S(2)}) %all-to-all-start) | async-done | bytes 655392 | tf_op jit(solution)/shard_map/all_to_all | solution.py:334
  34.3 10.6 %collective-permute-start = (bf16[48,640]{1,0:T(8,128)(2,1)S(1)}, bf16[48,640]{1,0:T(8,128)(2,1)S(1)}, u32[]{:S(2)}, u32[]{:S(2)}) collective-permute-start(bf16[48,640]{1,0:T(8,128)(2,1)S(1)} %bitcast.35), channel_id=1, source_target_pairs={{0,32},{32,0},{1,33},{33,1},{2,34},{34,2},{3,35},{35,3},{4,36},{36... | collective-permute-start | bytes 184328 | tf_op jit(solution)/shard_map/ppermute | solution.py:353
  47.5 3.5 %all-to-all-start.1 = ((bf16[8,48,640]{2,1,0:T(8,128)(2,1)}), bf16[8,48,640]{2,1,0:T(8,128)(2,1)S(1)}, u32[]{:S(2)}, u32[]{:S(2)}) async-start(bf16[8,48,640]{2,1,0:T(8,128)(2,1)} %broadcast_in_dim.59), calls=%async_computation.1 | async-start | bytes 983040 | tf_op jit(solution)/shard_map/all_to_all | solution.py:357
  51.0 12.6 %all-to-all-done.1 = bf16[8,48,640]{2,1,0:T(8,128)(2,1)S(1)} async-done(((bf16[8,48,640]{2,1,0:T(8,128)(2,1)}), bf16[8,48,640]{2,1,0:T(8,128)(2,1)S(1)}, u32[]{:S(2)}, u32[]{:S(2)}) %all-to-all-start.1) | async-done | bytes 491552 | tf_op jit(solution)/shard_map/all_to_all | solution.py:357
  64.7 3.5 %collective-permute-start.1 = (bf16[2,192,640]{2,1,0:T(8,128)(2,1)S(1)}, bf16[2,192,640]{2,1,0:T(8,128)(2,1)S(1)}, u32[]{:S(2)}, u32[]{:S(2)}) collective-permute-start(bf16[2,192,640]{2,1,0:T(8,128)(2,1)S(1)} %bitcast.25), channel_id=1, source_target_pairs={{0,8},{8,16},{16,24},{24,0},{1,9},{9,17},{17,25},{25,1},{2,10},{10... | collective-permute-start | bytes 1474568 | tf_op jit(solution)/shard_map/ppermute | solution.py:366
  68.3 3.5 %collective-permute-start.2 = (bf16[2,192,640]{2,1,0:T(8,128)(2,1)S(1)}, bf16[2,192,640]{2,1,0:T(8,128)(2,1)S(1)}, u32[]{:S(2)}, u32[]{:S(2)}) collective-permute-start(bf16[2,192,640]{2,1,0:T(8,128)(2,1)S(1)} %bitcast.26), channel_id=1, source_target_pairs={{0,24},{8,0},{16,8},{24,16},{1,25},{9,1},{17,9},{25,17},{2,26},{10... | collective-permute-start | bytes 1474568 | tf_op jit(solution)/shard_map/ppermute | solution.py:367
  72.1 4.4 %collective-permute-done.1.right = bf16[2,192,640]{2,1,0:T(8,128)(2,1)S(1)} collective-permute-done((bf16[2,192,640]{2,1,0:T(8,128)(2,1)S(1)}, bf16[2,192,640]{2,1,0:T(8,128)(2,1)S(1)}, u32[]{:S(2)}, u32[]{:S(2)}) %collective-permute-start.1) | collective-permute-done | bytes 491552 | tf_op jit(solution)/shard_map/ppermute | solution.py:366
  76.5 2.0 %collective-permute-start.3 = (bf16[192,640]{1,0:T(8,128)(2,1)S(1)}, bf16[192,640]{1,0:T(8,128)(2,1)S(1)}, u32[]{:S(2)}, u32[]{:S(2)}) collective-permute-start(bf16[192,640]{1,0:T(8,128)(2,1)S(1)} %slice_bitcast_fusion.1), channel_id=1, source_target_pairs={{0,8},{8,16},{16,24},{24,0},{1,9},{9,17},{17,25},{25,1},{2,10},{10... | collective-permute-start | bytes 737288 | tf_op jit(solution)/shard_map/ppermute | solution.py:368
  78.6 4.5 %collective-permute-start.4 = (bf16[192,640]{1,0:T(8,128)(2,1)S(1)}, bf16[192,640]{1,0:T(8,128)(2,1)S(1)}, u32[]{:S(2)}, u32[]{:S(2)}) collective-permute-start(bf16[192,640]{1,0:T(8,128)(2,1)S(1)} %slice_bitcast_fusion), channel_id=1, source_target_pairs={{0,24},{8,0},{16,8},{24,16},{1,25},{9,1},{17,9},{25,17},{2,26},{10... | collective-permute-start | bytes 737288 | tf_op jit(solution)/shard_map/ppermute | solution.py:369
  83.3 3.2 %shard_map.120 = (bf16[2,496,128]{2,1,0:T(8,128)(2,1)S(1)}, bf16[2,496,128]{2,1,0:T(8,128)(2,1)S(1)}, bf16[2,496,128]{2,1,0:T(8,128)(2,1)S(1)}) custom-call(s32[12]{0:T(128)S(1)} %concatenate.13.nums, bf16[2,192,640]{2,1,0:T(8,128)(2,1)S(1)} %bitcast.27, bf16[2,192,640]{2,1,0:T(8,128)(2,1)S(1)} %collective-permute-done.1.right, ...), custom_call_target="tpu_custom_call" | custom-call | flops 1006632960 | bytes 3886384 | tf_op jit(solution)/shard_map/pallas_call | solution.py:27
  86.5 7.9 %collective-permute-start.5 = (bf16[2,496,128]{2,1,0:T(8,128)(2,1)S(1)}, bf16[2,496,128]{2,1,0:T(8,128)(2,1)S(1)}, u32[]{:S(2)}, u32[]{:S(2)}) collective-permute-start(bf16[2,496,128]{2,1,0:T(8,128)(2,1)S(1)} %get-tuple-element.24), channel_id=1, source_target_pairs={{0,1},{1,0},{2,3},{3,2},{4,5},{5,4},{6,7},{7,6},{8,9},{9,8},{10,11... | collective-permute-start | bytes 761864 | tf_op jit(solution)/shard_map/ppermute | solution.py:388
  95.9 1.9 %collective-permute-start.6 = (bf16[2,496,128]{2,1,0:T(8,128)(2,1)S(1)}, bf16[2,496,128]{2,1,0:T(8,128)(2,1)S(1)}, u32[]{:S(2)}, u32[]{:S(2)}) collective-permute-start(bf16[2,496,128]{2,1,0:T(8,128)(2,1)S(1)} %get-tuple-element.25), channel_id=1, source_target_pairs={{0,1},{1,0},{2,3},{3,2},{4,5},{5,4},{6,7},{7,6},{8,9},{9,8},{10,11... | collective-permute-start | bytes 761864 | tf_op jit(solution)/shard_map/ppermute | solution.py:392
  100.0 3.0 %collective-permute-start.7 = (bf16[496,128]{1,0:T(8,128)(2,1)S(1)}, bf16[496,128]{1,0:T(8,128)(2,1)S(1)}, u32[]{:S(2)}, u32[]{:S(2)}) collective-permute-start(bf16[496,128]{1,0:T(8,128)(2,1)S(1)} %get-tuple-element.27), channel_id=1, source_target_pairs={{0,2},{2,0},{4,6},{6,4},{1,3},{3,1},{5,7},{7,5},{8,10},{10,8},{12,... | collective-permute-start | bytes 380936 | tf_op jit(solution)/shard_map/ppermute | solution.py:396
  103.1 4.7 %collective-permute-start.8 = (bf16[496,128]{1,0:T(8,128)(2,1)S(1)}, bf16[496,128]{1,0:T(8,128)(2,1)S(1)}, u32[]{:S(2)}, u32[]{:S(2)}) collective-permute-start(bf16[496,128]{1,0:T(8,128)(2,1)S(1)} %get-tuple-element.28), channel_id=1, source_target_pairs={{0,4},{2,6},{4,0},{6,2},{1,5},{3,7},{5,1},{7,3},{8,12},{10,14},{12... | collective-permute-start | bytes 380936 | tf_op jit(solution)/shard_map/ppermute | solution.py:396
  107.8 3.1 %collective-permute-start.9 = (bf16[496,128]{1,0:T(8,128)(2,1)S(1)}, bf16[496,128]{1,0:T(8,128)(2,1)S(1)}, u32[]{:S(2)}, u32[]{:S(2)}) collective-permute-start(bf16[496,128]{1,0:T(8,128)(2,1)S(1)} %get-tuple-element.29), channel_id=1, source_target_pairs={{0,6},{2,4},{4,2},{6,0},{1,7},{3,5},{5,3},{7,1},{8,14},{10,12},{12... | collective-permute-start | bytes 380936 | tf_op jit(solution)/shard_map/ppermute | solution.py:396
  110.9 3.2 %collective-permute-done.8.refs_2_ = bf16[496,128]{1,0:T(8,128)(2,1)S(1)} collective-permute-done((bf16[496,128]{1,0:T(8,128)(2,1)S(1)}, bf16[496,128]{1,0:T(8,128)(2,1)S(1)}, u32[]{:S(2)}, u32[]{:S(2)}) %collective-permute-start.8) | collective-permute-done | bytes 127008 | tf_op jit(solution)/shard_map/ppermute | solution.py:396
  114.0 2.0 %collective-permute-done.9.refs_3_ = bf16[496,128]{1,0:T(8,128)(2,1)S(1)} collective-permute-done((bf16[496,128]{1,0:T(8,128)(2,1)S(1)}, bf16[496,128]{1,0:T(8,128)(2,1)S(1)}, u32[]{:S(2)}, u32[]{:S(2)}) %collective-permute-start.9) | collective-permute-done | bytes 127008 | tf_op jit(solution)/shard_map/ppermute | solution.py:396
  116.5 21.1 %all_gather.3.every = bf16[3968,128]{1,0:T(8,128)(2,1)S(1)} all-gather(bf16[496,128]{1,0:T(8,128)(2,1)S(1)} %shard_map.123), channel_id=1, replica_groups=mesh['y'=8,'zh'=2,'x'=4,'zl'=4,'c'=2] {'zl','c'}, dimensions={0}, use_global_device_ids=true | all-gather | bytes 1142784 | tf_op jit(solution)/shard_map/all_gather | solution.py:407
  137.6 4.0 %shard_map.124 = (bf16[4,272,640]{2,1,0:T(8,128)(2,1)S(1)}, bf16[16,640]{1,0:T(8,128)(2,1)S(1)}) custom-call(s32[12]{0:T(128)S(1)} %concatenate.13.nums, bf16[2,192,640]{2,1,0:T(8,128)(2,1)S(1)} %bitcast.28, bf16[2,192,640]{2,1,0:T(8,128)(2,1)S(1)} %collective-permute-done.1.right, bf16[2,192,640]{2,1,0:T(8,128)(2,1)S(1)} %collective-permute-done.2.left, ...), custom_call_target="tpu_custom_call" | custom-call | flops 1258291200 | bytes 4949296 | tf_op jit(solution)/shard_map/pallas_call | solution.py:27
  141.7 20.6 %all_to_all.28.parts = bf16[4,272,640]{2,1,0:T(8,128)(2,1)S(1)} all-to-all(bf16[4,272,640]{2,1,0:T(8,128)(2,1)S(1)} %get-tuple-element.30), channel_id=1, replica_groups=mesh['y'=8,'zh'=2,'x'=4,'zl'=4,'c'=2] {'x'}, dimensions={0} | all-to-all | bytes 2785280 | tf_op jit(solution)/shard_map/all_to_all | solution.py:418
  163.2 7.6 %all-to-all-start.3 = ((bf16[16,16,768]{2,1,0:T(8,128)(2,1)}), bf16[16,16,768]{2,1,0:T(8,128)(2,1)S(1)}, u32[]{:S(2)}, u32[]{:S(2)}) async-start(bf16[16,16,768]{2,1,0:T(8,128)(2,1)} %shard_map.125), calls=%async_computation.3 | async-start | bytes 786432 | tf_op jit(solution)/shard_map/all_to_all | solution.py:422
  170.8 2.6 %shard_map.127 = (bf16[216,640]{1,0:T(8,128)(2,1)}, bf16[216,640]{1,0:T(8,128)(2,1)}, bf16[216,640]{1,0:T(8,128)(2,1)}) custom-call(bf16[2,192,640]{2,1,0:T(8,128)(2,1)S(1)} %bitcast.29, bf16[2,192,640]{2,1,0:T(8,128)(2,1)S(1)} %collective-permute-done.1.right, bf16[2,192,640]{2,1,0:T(8,128)(2,1)S(1)} %collective-permute-done.2.left, ...), custom_call_target="tpu_custom_call" | custom-call | flops 754974720 | bytes 3812608 | tf_op jit(solution)/shard_map/pallas_call | solution.py:27
  173.5 13.7 %all-to-all-done.3.parts = bf16[16,16,768]{2,1,0:T(8,128)(2,1)S(1)} async-done(((bf16[16,16,768]{2,1,0:T(8,128)(2,1)}), bf16[16,16,768]{2,1,0:T(8,128)(2,1)S(1)}, u32[]{:S(2)}, u32[]{:S(2)}) %all-to-all-start.3) | async-done | bytes 393248 | tf_op jit(solution)/shard_map/all_to_all | solution.py:422
  (60 shorter events, 15.2 us)
Async XLA Ops:
  0.6 1.0 copy-start
  1.6 1.0 copy-start.1
  2.6 0.7 copy-start.6
  3.2 12.3 %copy-start.10 = (s32[16]{0:T(128)S(1)}, s32[16]{0:T(128)}, u32[]{:S(2)}) copy-start(s32[16]{0:T(128)} %param.10) | copy-start | bytes 196
  3.2 12.5 %copy-start.7 = (s32[4]{0:T(128)S(1)}, s32[4]{0:T(128)}, u32[]{:S(2)}) copy-start(s32[4]{0:T(128)} %live.1) | copy-start | bytes 52
  5.0 29.2 %all-to-all-start = ((bf16[32,16,640]{2,1,0:T(8,128)(2,1)}), bf16[32,16,640]{2,1,0:T(8,128)(2,1)S(1)}, u32[]{:S(2)}, u32[]{:S(2)}) async-start(bf16[32,16,640]{2,1,0:T(8,128)(2,1)} %bitcast.5), calls=%async_computation | async-start | bytes 1310720 | tf_op jit(solution)/shard_map/all_to_all | solution.py:334
  34.3 12.3 %collective-permute-start = (bf16[48,640]{1,0:T(8,128)(2,1)S(1)}, bf16[48,640]{1,0:T(8,128)(2,1)S(1)}, u32[]{:S(2)}, u32[]{:S(2)}) collective-permute-start(bf16[48,640]{1,0:T(8,128)(2,1)S(1)} %bitcast.35), channel_id=1, source_target_pairs={{0,32},{32,0},{1,33},{33,1},{2,34},{34,2},{3,35},{35,3},{4,36},{36... | collective-permute-start | bytes 184328 | tf_op jit(solution)/shard_map/ppermute | solution.py:353
  47.5 16.2 %all-to-all-start.1 = ((bf16[8,48,640]{2,1,0:T(8,128)(2,1)}), bf16[8,48,640]{2,1,0:T(8,128)(2,1)S(1)}, u32[]{:S(2)}, u32[]{:S(2)}) async-start(bf16[8,48,640]{2,1,0:T(8,128)(2,1)} %broadcast_in_dim.59), calls=%async_computation.1 | async-start | bytes 983040 | tf_op jit(solution)/shard_map/all_to_all | solution.py:357
  63.7 8.1 %copy-start.8 = (bf16[216,640]{1,0:T(8,128)(2,1)S(1)}, bf16[216,640]{1,0:T(8,128)(2,1)}, u32[]{:S(2)}) copy-start(bf16[216,640]{1,0:T(8,128)(2,1)} %param.14) | copy-start | bytes 829444
  63.7 8.2 %copy-start.9 = (bf16[640]{0:T(1024)(128)(2,1)S(1)}, bf16[640]{0:T(1024)(128)(2,1)}, u32[]{:S(2)}) copy-start(bf16[640]{0:T(1024)(128)(2,1)} %param.15) | copy-start | bytes 3844
  64.7 18.3 %copy-start.2 = (bf16[640,216]{0,1:T(8,128)(2,1)S(1)}, bf16[640,216]{0,1:T(8,128)(2,1)}, u32[]{:S(2)}) copy-start(bf16[640,216]{0,1:T(8,128)(2,1)} %param.13) | copy-start | bytes 829444
  64.7 18.3 %copy-start.4 = (bf16[640,216]{0,1:T(8,128)(2,1)S(1)}, bf16[640,216]{0,1:T(8,128)(2,1)}, u32[]{:S(2)}) copy-start(bf16[640,216]{0,1:T(8,128)(2,1)} %param.12) | copy-start | bytes 829444
  64.7 11.7 %collective-permute-start.1 = (bf16[2,192,640]{2,1,0:T(8,128)(2,1)S(1)}, bf16[2,192,640]{2,1,0:T(8,128)(2,1)S(1)}, u32[]{:S(2)}, u32[]{:S(2)}) collective-permute-start(bf16[2,192,640]{2,1,0:T(8,128)(2,1)S(1)} %bitcast.25), channel_id=1, source_target_pairs={{0,8},{8,16},{16,24},{24,0},{1,9},{9,17},{17,25},{25,1},{2,10},{10... | collective-permute-start | bytes 1474568 | tf_op jit(solution)/shard_map/ppermute | solution.py:366
  68.3 10.3 %collective-permute-start.2 = (bf16[2,192,640]{2,1,0:T(8,128)(2,1)S(1)}, bf16[2,192,640]{2,1,0:T(8,128)(2,1)S(1)}, u32[]{:S(2)}, u32[]{:S(2)}) collective-permute-start(bf16[2,192,640]{2,1,0:T(8,128)(2,1)S(1)} %bitcast.26), channel_id=1, source_target_pairs={{0,24},{8,0},{16,8},{24,16},{1,25},{9,1},{17,9},{25,17},{2,26},{10... | collective-permute-start | bytes 1474568 | tf_op jit(solution)/shard_map/ppermute | solution.py:367
  76.5 17.9 %collective-permute-start.3 = (bf16[192,640]{1,0:T(8,128)(2,1)S(1)}, bf16[192,640]{1,0:T(8,128)(2,1)S(1)}, u32[]{:S(2)}, u32[]{:S(2)}) collective-permute-start(bf16[192,640]{1,0:T(8,128)(2,1)S(1)} %slice_bitcast_fusion.1), channel_id=1, source_target_pairs={{0,8},{8,16},{16,24},{24,0},{1,9},{9,17},{17,25},{25,1},{2,10},{10... | collective-permute-start | bytes 737288 | tf_op jit(solution)/shard_map/ppermute | solution.py:368
  78.6 15.8 %collective-permute-start.4 = (bf16[192,640]{1,0:T(8,128)(2,1)S(1)}, bf16[192,640]{1,0:T(8,128)(2,1)S(1)}, u32[]{:S(2)}, u32[]{:S(2)}) collective-permute-start(bf16[192,640]{1,0:T(8,128)(2,1)S(1)} %slice_bitcast_fusion), channel_id=1, source_target_pairs={{0,24},{8,0},{16,8},{24,16},{1,25},{9,1},{17,9},{25,17},{2,26},{10... | collective-permute-start | bytes 737288 | tf_op jit(solution)/shard_map/ppermute | solution.py:369
  86.5 11.4 %collective-permute-start.5 = (bf16[2,496,128]{2,1,0:T(8,128)(2,1)S(1)}, bf16[2,496,128]{2,1,0:T(8,128)(2,1)S(1)}, u32[]{:S(2)}, u32[]{:S(2)}) collective-permute-start(bf16[2,496,128]{2,1,0:T(8,128)(2,1)S(1)} %get-tuple-element.24), channel_id=1, source_target_pairs={{0,1},{1,0},{2,3},{3,2},{4,5},{5,4},{6,7},{7,6},{8,9},{9,8},{10,11... | collective-permute-start | bytes 761864 | tf_op jit(solution)/shard_map/ppermute | solution.py:388
  95.9 3.4 %collective-permute-start.6 = (bf16[2,496,128]{2,1,0:T(8,128)(2,1)S(1)}, bf16[2,496,128]{2,1,0:T(8,128)(2,1)S(1)}, u32[]{:S(2)}, u32[]{:S(2)}) collective-permute-start(bf16[2,496,128]{2,1,0:T(8,128)(2,1)S(1)} %get-tuple-element.25), channel_id=1, source_target_pairs={{0,1},{1,0},{2,3},{3,2},{4,5},{5,4},{6,7},{7,6},{8,9},{9,8},{10,11... | collective-permute-start | bytes 761864 | tf_op jit(solution)/shard_map/ppermute | solution.py:392
  99.3 38.3 %copy-start.3 = (bf16[640,216]{0,1:T(8,128)(2,1)S(1)}, bf16[640,216]{0,1:T(8,128)(2,1)}, u32[]{:S(2)}) copy-start(bf16[640,216]{0,1:T(8,128)(2,1)} %param.13) | copy-start | bytes 829444
  99.3 38.3 %copy-start.5 = (bf16[640,216]{0,1:T(8,128)(2,1)S(1)}, bf16[640,216]{0,1:T(8,128)(2,1)}, u32[]{:S(2)}) copy-start(bf16[640,216]{0,1:T(8,128)(2,1)} %param.12) | copy-start | bytes 829444
  100.0 10.8 %collective-permute-start.7 = (bf16[496,128]{1,0:T(8,128)(2,1)S(1)}, bf16[496,128]{1,0:T(8,128)(2,1)S(1)}, u32[]{:S(2)}, u32[]{:S(2)}) collective-permute-start(bf16[496,128]{1,0:T(8,128)(2,1)S(1)} %get-tuple-element.27), channel_id=1, source_target_pairs={{0,2},{2,0},{4,6},{6,4},{1,3},{3,1},{5,7},{7,5},{8,10},{10,8},{12,... | collective-permute-start | bytes 380936 | tf_op jit(solution)/shard_map/ppermute | solution.py:396
  103.1 10.9 %collective-permute-start.8 = (bf16[496,128]{1,0:T(8,128)(2,1)S(1)}, bf16[496,128]{1,0:T(8,128)(2,1)S(1)}, u32[]{:S(2)}, u32[]{:S(2)}) collective-permute-start(bf16[496,128]{1,0:T(8,128)(2,1)S(1)} %get-tuple-element.28), channel_id=1, source_target_pairs={{0,4},{2,6},{4,0},{6,2},{1,5},{3,7},{5,1},{7,3},{8,12},{10,14},{12... | collective-permute-start | bytes 380936 | tf_op jit(solution)/shard_map/ppermute | solution.py:396
  107.8 8.2 %collective-permute-start.9 = (bf16[496,128]{1,0:T(8,128)(2,1)S(1)}, bf16[496,128]{1,0:T(8,128)(2,1)S(1)}, u32[]{:S(2)}, u32[]{:S(2)}) collective-permute-start(bf16[496,128]{1,0:T(8,128)(2,1)S(1)} %get-tuple-element.29), channel_id=1, source_target_pairs={{0,6},{2,4},{4,2},{6,0},{1,7},{3,5},{5,3},{7,1},{8,14},{10,12},{12... | collective-permute-start | bytes 380936 | tf_op jit(solution)/shard_map/ppermute | solution.py:396
  163.2 23.9 %all-to-all-start.3 = ((bf16[16,16,768]{2,1,0:T(8,128)(2,1)}), bf16[16,16,768]{2,1,0:T(8,128)(2,1)S(1)}, u32[]{:S(2)}, u32[]{:S(2)}) async-start(bf16[16,16,768]{2,1,0:T(8,128)(2,1)} %shard_map.125), calls=%async_computation.3 | async-start | bytes 786432 | tf_op jit(solution)/shard_map/all_to_all | solution.py:422
